TPU v7x, 32 devices: a whole 2x2x4 slice. The times are simulated.
32 devices in a mesh: dp: 8 (over z, y), seq: 4 (over x, core).
Axes of the slice: x: 2, y: 2, z: 4, core: 2. Of those that a mesh axis runs over, the one named last changes fastest.
Arguments:
- tokens: bfloat16 [16, 1024, 768], P('dp', 'seq'), may hold values from -6 to 6
- segment_ids: int32 [16, 1024], P('dp'), may hold values from 0 to 7, never falling along the last dimension, each value on 1 to 512 neighbouring positions
- w_qkv: bfloat16 [768, 2304], P(('dp', 'seq')), may hold values from -0.21875 to 0.21875
- b_qkv: bfloat16 [2304], P(('dp', 'seq')), may hold values from -1.796875 to 1.796875
- w_out: bfloat16 [768, 768], P(('dp', 'seq')), may hold values from -0.625 to 0.625
- b_out: bfloat16 [768], P(('dp', 'seq')), may hold values from -4 to 4
- ln1_gain: bfloat16 [768], P(('dp', 'seq')), may hold values from 0.25 to 1.75
- ln1_bias: bfloat16 [768], P(('dp', 'seq')), may hold values from -1.796875 to 1.796875
- w_in: bfloat16 [768, 3072], P(('dp', 'seq')), may hold values from -0.21875 to 0.21875
- b_in: bfloat16 [3072], P(('dp', 'seq')), may hold values from -1.796875 to 1.796875
- w_back: bfloat16 [3072, 768], P(('dp', 'seq')), may hold values from -0.15625 to 0.15625
- b_back: bfloat16 [768], P(('dp', 'seq')), may hold values from -1.796875 to 1.796875
- ln2_gain: bfloat16 [768], P(('dp', 'seq')), may hold values from 0.25 to 1.75
- ln2_bias: bfloat16 [768], P(('dp', 'seq')), may hold values from -1.796875 to 1.796875
- out_grad: bfloat16 [16, 1024, 768], P('dp', 'seq'), may hold values from -6 to 6
Outputs:
- layer_out: bfloat16 [16, 1024, 768], P('dp', 'seq')
- input_grad: float32 [16, 1024, 768], P('dp', 'seq')
- w_qkv_grad: float32 [768, 2304], P(('dp', 'seq'))
- b_qkv_grad: float32 [2304], P(('dp', 'seq'))
- w_out_grad: float32 [768, 768], P(('dp', 'seq'))
- b_out_grad: float32 [768], P(('dp', 'seq'))
- ln1_gain_grad: float32 [768], P(('dp', 'seq'))
- ln1_bias_grad: float32 [768], P(('dp', 'seq'))
- w_in_grad: float32 [768, 3072], P(('dp', 'seq'))
- b_in_grad: float32 [3072], P(('dp', 'seq'))
- w_back_grad: float32 [3072, 768], P(('dp', 'seq'))
- b_back_grad: float32 [768], P(('dp', 'seq'))
- ln2_gain_grad: float32 [768], P(('dp', 'seq'))
- ln2_bias_grad: float32 [768], P(('dp', 'seq'))
Inputs may be any that keep to these rules, and one draw needn't show every extreme that they name: `segment_ids`: along each sequence the ids never fall; a document holds 1 to 512 tokens, and in every sequence one holds exactly 512.
All inputs are finite; a program needn't handle non-finite values.
Results may differ from a plain program's by a relative error of at most 0.034.
Values may be sent and summed in bfloat16 or wider, within the bound.
A program may use at most 320 MiB of HBM per device.

v0:
```python
import jax
import jax.numpy as jnp
from jax import lax
from jax.sharding import PartitionSpec as P

D = 768
HEADS = 12
HD = 64
FF = 3072


EPSILON = 1e-06


def layer_norm(values, gain_vec, shift_vec):
    center = values - jnp.mean(values, axis=-1, keepdims=True)
    spread = jnp.mean(center * center, axis=-1, keepdims=True)
    return center * lax.rsqrt(spread + EPSILON) * gain_vec + shift_vec


def gelu_exact(values):
    return jax.nn.gelu(values, approximate=False)


def rotary_tables(segments, offset, row_count):
    length = segments.shape[0]
    places = jnp.arange(length, dtype=jnp.int32)
    change = jnp.concatenate([jnp.ones((1,), dtype=bool), segments[1:] != segments[:-1]])
    starts = lax.cummax(jnp.where(change, places, jnp.zeros_like(places)), axis=0)
    position = (places - starts).astype(jnp.float32)
    half_size = HD // 2
    inverse = 10000.0 ** (-2.0 * jnp.arange(half_size, dtype=jnp.float32) / HD)
    angles = position[:, None] * inverse[None, :]
    angles = lax.dynamic_slice_in_dim(angles, offset, row_count, 0)
    return (jnp.cos(angles), jnp.sin(angles))


def rotate(values, cos_part, sin_part):
    row_count = values.shape[0]
    paired = values.reshape(row_count, HEADS, HD // 2, 2)
    even_part = paired[..., 0]
    odd_part = paired[..., 1]
    cos_wide = cos_part[:, None, :]
    sin_wide = sin_part[:, None, :]
    turned = jnp.stack(
        [even_part * cos_wide - odd_part * sin_wide, even_part * sin_wide + odd_part * cos_wide],
        axis=-1,
    )
    return turned.reshape(row_count, HEADS * HD)


def masked_scores(query_rot, key_all, same_doc):
    query_heads = query_rot.reshape(query_rot.shape[0], HEADS, HD)
    key_heads = key_all.reshape(key_all.shape[0], HEADS, HD)
    raw_scores = jnp.einsum(
        "qhd,khd->hqk", query_heads, key_heads, preferred_element_type=jnp.float32
    )
    return jnp.where(same_doc[None], raw_scores * HD ** (-0.5), -1e30)


def fetch_attention(local_set):
    return (
        lax.all_gather(local_set[0], ("dp", "seq"), axis=0, tiled=True),
        lax.all_gather(local_set[1], ("dp", "seq"), axis=0, tiled=True),
        lax.all_gather(local_set[2], ("dp", "seq"), axis=0, tiled=True),
        lax.all_gather(local_set[3], ("dp", "seq"), axis=0, tiled=True),
        lax.all_gather(local_set[4], ("dp", "seq"), axis=0, tiled=True),
        lax.all_gather(local_set[5], ("dp", "seq"), axis=0, tiled=True),
    )


def fetch_feed(local_set):
    return (
        lax.all_gather(local_set[0], ("dp", "seq"), axis=0, tiled=True),
        lax.all_gather(local_set[1], ("dp", "seq"), axis=0, tiled=True),
        lax.all_gather(local_set[2], ("dp", "seq"), axis=0, tiled=True),
        lax.all_gather(local_set[3], ("dp", "seq"), axis=0, tiled=True),
        lax.all_gather(local_set[4], ("dp", "seq"), axis=0, tiled=True),
        lax.all_gather(local_set[5], ("dp", "seq"), axis=0, tiled=True),
    )


def forward_pass(tok_rows, seq_ids, attention_set, feed_set):
    w_qkv, b_qkv, w_out, b_out, gain_one, shift_one = attention_set
    w_in, b_in, w_back, b_back, gain_two, shift_two = feed_set
    row_count = tok_rows.shape[0]
    offset = lax.axis_index("seq") * row_count
    cos_part, sin_part = rotary_tables(seq_ids, offset, row_count)
    own_ids = lax.dynamic_slice_in_dim(seq_ids, offset, row_count, 0)
    joined_qkv = jnp.dot(tok_rows, w_qkv, preferred_element_type=jnp.float32) + b_qkv.astype(
        jnp.float32
    )
    query_rot = rotate(joined_qkv[:, :D], cos_part, sin_part).astype(jnp.bfloat16)
    key_rot = rotate(joined_qkv[:, D : 2 * D], cos_part, sin_part).astype(jnp.bfloat16)
    value_own = joined_qkv[:, 2 * D :].astype(jnp.bfloat16)
    key_all, value_all = (
        lax.all_gather(key_rot, "seq", axis=0, tiled=True),
        lax.all_gather(value_own, "seq", axis=0, tiled=True),
    )
    same_doc = own_ids[:, None] == seq_ids[None, :]
    scores = masked_scores(query_rot, key_all, same_doc)
    highest = jnp.max(scores, axis=-1, keepdims=True)
    exponent = jnp.exp(scores - highest)
    row_total = jnp.sum(exponent, axis=-1, keepdims=True)
    attention = exponent / row_total
    log_total = highest + jnp.log(row_total)
    value_heads = value_all.reshape(value_all.shape[0], HEADS, HD)
    mixed_out = jnp.einsum(
        "hqk,khd->qhd",
        attention.astype(jnp.bfloat16),
        value_heads,
        preferred_element_type=jnp.float32,
    )
    mixed_out = mixed_out.reshape(row_count, D).astype(jnp.bfloat16)
    branch = jnp.dot(mixed_out, w_out, preferred_element_type=jnp.float32) + b_out.astype(
        jnp.float32
    )
    first_sum = tok_rows.astype(jnp.float32) + branch
    normed = layer_norm(first_sum, gain_one.astype(jnp.float32), shift_one.astype(jnp.float32))
    normed_low = normed.astype(jnp.bfloat16)
    inner_act = jnp.dot(normed_low, w_in, preferred_element_type=jnp.float32) + b_in.astype(
        jnp.float32
    )
    active = gelu_exact(inner_act).astype(jnp.bfloat16)
    second = jnp.dot(active, w_back, preferred_element_type=jnp.float32) + b_back.astype(
        jnp.float32
    )
    second_sum = normed + second
    result = layer_norm(
        second_sum, gain_two.astype(jnp.float32), shift_two.astype(jnp.float32)
    ).astype(jnp.bfloat16)
    kept_state = (
        cos_part,
        sin_part,
        same_doc,
        own_ids,
        query_rot,
        key_rot,
        value_own,
        key_all,
        value_all,
        log_total,
        mixed_out,
        first_sum,
        normed_low,
        inner_act,
        active,
        second_sum,
    )
    return (result, kept_state)


def backward_pass(tok_rows, grad_rows, kept_state, attention_set, feed_set):
    w_qkv, b_qkv, w_out, b_out, gain_one, shift_one = attention_set
    w_in, b_in, w_back, b_back, gain_two, shift_two = feed_set
    (
        cos_part,
        sin_part,
        same_doc,
        own_ids,
        query_rot,
        key_rot,
        value_own,
        key_all,
        value_all,
        log_total,
        mixed_out,
        first_sum,
        normed_low,
        inner_act,
        active,
        second_sum,
    ) = kept_state
    row_count = tok_rows.shape[0]
    key_count = key_all.shape[0]
    unused_out, pull_back = jax.vjp(
        layer_norm, second_sum, gain_two.astype(jnp.float32), shift_two.astype(jnp.float32)
    )
    d_second_sum, d_gain_two, d_shift_two = pull_back(grad_rows.astype(jnp.float32))
    d_second = d_second_sum.astype(jnp.bfloat16)
    d_b_back = jnp.sum(d_second.astype(jnp.float32), axis=0)
    d_w_back = jnp.einsum("qf,qd->fd", active, d_second, preferred_element_type=jnp.float32)
    d_active = jnp.einsum("qd,fd->qf", d_second, w_back, preferred_element_type=jnp.float32)
    unused_gelu, pull_gelu = jax.vjp(gelu_exact, inner_act)
    d_inner = pull_gelu(d_active)[0].astype(jnp.bfloat16)
    d_b_in = jnp.sum(d_inner.astype(jnp.float32), axis=0)
    d_w_in = jnp.einsum("qd,qf->df", normed_low, d_inner, preferred_element_type=jnp.float32)
    d_normed = d_second_sum + jnp.einsum(
        "qf,df->qd", d_inner, w_in, preferred_element_type=jnp.float32
    )
    unused_norm, pull_norm = jax.vjp(
        layer_norm, first_sum, gain_one.astype(jnp.float32), shift_one.astype(jnp.float32)
    )
    d_first_sum, d_gain_one, d_shift_one = pull_norm(d_normed)
    d_branch = d_first_sum.astype(jnp.bfloat16)
    d_b_out = jnp.sum(d_branch.astype(jnp.float32), axis=0)
    d_w_out = jnp.einsum("qd,qe->de", mixed_out, d_branch, preferred_element_type=jnp.float32)
    d_mixed = jnp.einsum("qe,de->qd", d_branch, w_out, preferred_element_type=jnp.float32).astype(
        jnp.bfloat16
    )
    scores = masked_scores(query_rot, key_all, same_doc)
    attention = jnp.exp(scores - log_total)
    d_heads = d_mixed.reshape(row_count, HEADS, HD)
    query_heads = query_rot.reshape(row_count, HEADS, HD)
    key_heads = key_all.reshape(key_count, HEADS, HD)
    value_heads = value_all.reshape(key_count, HEADS, HD)
    d_attention = jnp.einsum(
        "qhd,khd->hqk", d_heads, value_heads, preferred_element_type=jnp.float32
    )
    inner_sum = jnp.sum(d_attention * attention, axis=-1, keepdims=True)
    d_scores = (attention * (d_attention - inner_sum) * HD ** (-0.5)).astype(jnp.bfloat16)
    d_query = jnp.einsum(
        "hqk,khd->qhd", d_scores, key_heads, preferred_element_type=jnp.float32
    ).reshape(row_count, D)
    d_value = jnp.einsum(
        "hqk,qhd->khd", attention.astype(jnp.bfloat16), d_heads, preferred_element_type=jnp.float32
    ).reshape(key_count, D)
    d_key = jnp.einsum(
        "hqk,qhd->khd", d_scores, query_heads, preferred_element_type=jnp.float32
    ).reshape(key_count, D)
    d_key_own, d_value_own = (
        lax.psum_scatter(d_key.astype(jnp.bfloat16), "seq", scatter_dimension=0, tiled=True).astype(
            jnp.float32
        ),
        lax.psum_scatter(
            d_value.astype(jnp.bfloat16), "seq", scatter_dimension=0, tiled=True
        ).astype(jnp.float32),
    )
    d_joined = jnp.concatenate(
        [rotate(d_query, cos_part, -sin_part), rotate(d_key_own, cos_part, -sin_part), d_value_own],
        axis=1,
    ).astype(jnp.bfloat16)
    d_b_qkv = jnp.sum(d_joined.astype(jnp.float32), axis=0)
    d_w_qkv = jnp.einsum("qd,qe->de", tok_rows, d_joined, preferred_element_type=jnp.float32)
    d_tokens = (
        jnp.einsum("qe,de->qd", d_joined, w_qkv, preferred_element_type=jnp.float32) + d_first_sum
    )
    grad_set = (
        d_w_qkv,
        d_b_qkv,
        d_w_out,
        d_b_out,
        d_gain_one,
        d_shift_one,
        d_w_in,
        d_b_in,
        d_w_back,
        d_b_back,
        d_gain_two,
        d_shift_two,
    )
    return (grad_set, d_tokens)


def on_device(
    tokens,
    segment_ids,
    w_qkv,
    b_qkv,
    w_out,
    b_out,
    ln1_gain,
    ln1_bias,
    w_in,
    b_in,
    w_back,
    b_back,
    ln2_gain,
    ln2_bias,
    out_grad,
):
    local_attention = (w_qkv, b_qkv, w_out, b_out, ln1_gain, ln1_bias)
    local_feed = (w_in, b_in, w_back, b_back, ln2_gain, ln2_bias)
    start_sums = (
        jnp.zeros((D, 3 * D), jnp.float32),
        jnp.zeros((3 * D,), jnp.float32),
        jnp.zeros((D, D), jnp.float32),
        jnp.zeros((D,), jnp.float32),
        jnp.zeros((D,), jnp.float32),
        jnp.zeros((D,), jnp.float32),
        jnp.zeros((D, FF), jnp.float32),
        jnp.zeros((FF,), jnp.float32),
        jnp.zeros((FF, D), jnp.float32),
        jnp.zeros((D,), jnp.float32),
        jnp.zeros((D,), jnp.float32),
        jnp.zeros((D,), jnp.float32),
    )

    def one_micro(running, inputs):
        tok_rows, seq_ids, grad_rows = inputs
        attention_set = tuple(fetch_attention(local_attention))
        feed_set = tuple(fetch_feed(local_feed))
        result, kept_state = forward_pass(tok_rows, seq_ids, attention_set, feed_set)
        attention_set = tuple(fetch_attention(local_attention))
        feed_set = tuple(fetch_feed(local_feed))
        grad_set, d_tokens = backward_pass(tok_rows, grad_rows, kept_state, attention_set, feed_set)
        running = jax.tree.map(jnp.add, running, tuple(grad_set))
        return (running, (result, d_tokens))

    running, outputs = lax.scan(one_micro, start_sums, (tokens, segment_ids, out_grad))
    layer_out, input_grad = outputs
    running = (
        lax.psum_scatter(running[0], ("dp", "seq"), scatter_dimension=0, tiled=True),
        lax.psum_scatter(running[1], ("dp", "seq"), scatter_dimension=0, tiled=True),
        lax.psum_scatter(running[2], ("dp", "seq"), scatter_dimension=0, tiled=True),
        lax.psum_scatter(running[3], ("dp", "seq"), scatter_dimension=0, tiled=True),
        lax.psum_scatter(running[4], ("dp", "seq"), scatter_dimension=0, tiled=True),
        lax.psum_scatter(running[5], ("dp", "seq"), scatter_dimension=0, tiled=True),
        lax.psum_scatter(running[6], ("dp", "seq"), scatter_dimension=0, tiled=True),
        lax.psum_scatter(running[7], ("dp", "seq"), scatter_dimension=0, tiled=True),
        lax.psum_scatter(running[8], ("dp", "seq"), scatter_dimension=0, tiled=True),
        lax.psum_scatter(running[9], ("dp", "seq"), scatter_dimension=0, tiled=True),
        lax.psum_scatter(running[10], ("dp", "seq"), scatter_dimension=0, tiled=True),
        lax.psum_scatter(running[11], ("dp", "seq"), scatter_dimension=0, tiled=True),
    )
    return (layer_out, input_grad) + tuple(running)


def solution(mesh):
    in_specs = (
        P("dp", "seq", None),
        P("dp", None),
        P(("dp", "seq"), None),
        P(("dp", "seq")),
        P(("dp", "seq"), None),
        P(("dp", "seq")),
        P(("dp", "seq")),
        P(("dp", "seq")),
        P(("dp", "seq"), None),
        P(("dp", "seq")),
        P(("dp", "seq"), None),
        P(("dp", "seq")),
        P(("dp", "seq")),
        P(("dp", "seq")),
        P("dp", "seq", None),
    )
    out_specs = (
        P("dp", "seq", None),
        P("dp", "seq", None),
        P(("dp", "seq"), None),
        P(("dp", "seq")),
        P(("dp", "seq"), None),
        P(("dp", "seq")),
        P(("dp", "seq")),
        P(("dp", "seq")),
        P(("dp", "seq"), None),
        P(("dp", "seq")),
        P(("dp", "seq"), None),
        P(("dp", "seq")),
        P(("dp", "seq")),
        P(("dp", "seq")),
    )
    return jax.shard_map(
        on_device, mesh=mesh, in_specs=in_specs, out_specs=out_specs, check_vma=False
    )
```

profile of v0, /device:TPU:0, one launch (start us, length us, event | category | flops | bytes accessed | tf_op | source)
XLA Modules:
  0.0 1414.3 jit_solution(8566034862520147492)
XLA Ops:
  8.1 886.3 %while.40 = (s32[]{:T(128)}, f32[768,2304]{1,0:T(8,128)}, f32[2304]{0:T(1024)}, f32[768,768]{1,0:T(8,128)}, f32[768]{0:T(1024)}, /*index=5*/f32[768]{0:T(1024)},...) while((s32[]{:T(128)}, f32[768,2304]{1,0:T(8,128)}, ...), condition=%wide.region_24.25_spmd.clone, body=%wide.region_0.24_spmd.clone.sunk | while | flops 13511357440 | bytes 553063680 | solution.py:300
  16.1 42.9 %all-reduce.27 = (bf16[2304]{0:T(1024)(128)(2,1)S(1)}, bf16[3072]{0:T(1024)(128)(2,1)S(1)}, bf16[768]{0:T(1024)(128)(2,1)S(1)}, bf16[768]{0:T(1024)(128)(2,1)S(1...) all-reduce(bf16[2304]{0:T(1024)(128)(2,1)S(1)} %dynamic-update-slic, ...), channel_id=1, replica_groups=mesh['dp'=8,'seq'=4] {'dp','seq'}, use_global_device_ids=true, to_apply=%add | all-reduce | flops 9984 | bytes 39936 | tf_op jit(solution)/shard_map/while
  59.1 16.1 %all-gather.7.cloned.1.call-done = bf16[768,2304]{1,0:T(8,128)(2,1)} async-done(((bf16[24,2304]{1,0:T(8,128)(2,1)}), bf16[768,2304]{1,0:T(8,128)(2,1)}) %all-gather.7.cloned.1.call-update) | async-done | bytes 3538960 | tf_op jit(solution)/shard_map/while/body/eval_jaxpr/all_gather | solution.py:63
  92.7 6.6 all-gather.9.cloned.1.call-done
  101.0 19.7 %all-gather.11.cloned.1.call-done = bf16[1024,768]{0,1:T(8,128)(2,1)} async-done(((bf16[256,768]{0,1:T(8,128)(2,1)}), bf16[1024,768]{0,1:T(8,128)(2,1)}) %all-gather.11.cloned.1.call-update) | async-done | bytes 1572880 | tf_op jit(solution)/shard_map/while/body/eval_jaxpr/all_gather | solution.py:97
  132.9 44.7 %all-gather.13.cloned.1.call-done = bf16[768,768]{1,0:T(8,128)(2,1)} async-done(((bf16[24,768]{1,0:T(8,128)(2,1)}), bf16[768,768]{1,0:T(8,128)(2,1)}) %all-gather.13.cloned.1.call-update) | async-done | bytes 1179664 | tf_op jit(solution)/shard_map/while/body/eval_jaxpr/all_gather | solution.py:65
  180.4 62.5 %all-gather.15.cloned.1.call-done = bf16[768,3072]{1,0:T(8,128)(2,1)} async-done(((bf16[24,3072]{1,0:T(8,128)(2,1)}), bf16[768,3072]{1,0:T(8,128)(2,1)}) %all-gather.15.cloned.1.call-update) | async-done | bytes 4718608 | tf_op jit(solution)/shard_map/while/body/eval_jaxpr/all_gather | solution.py:74
  242.9 12.0 multiply_convert_fusion.3
  254.9 53.2 %all-gather.17.cloned.1.call-done = bf16[3072,768]{1,0:T(8,128)(2,1)} async-done(((bf16[96,768]{1,0:T(8,128)(2,1)}), bf16[3072,768]{1,0:T(8,128)(2,1)}) %all-gather.17.cloned.1.call-update) | async-done | bytes 4718608 | tf_op jit(solution)/shard_map/while/body/eval_jaxpr/all_gather | solution.py:76
  325.3 7.3 fusion.223
  332.6 35.0 %fusion.224 = bf16[12,64,1024]{2,1,0:T(8,128)(2,1)} fusion(bf16[256,12,64]{0,2,1:T(8,128)(2,1)} %copy-done.16, f32[12,256,1024]{2,1,0:T(8,128)} %fusion.223, f32[12,256,1024]{2,1,0:T(8,128)} %copy-done, f32[12,256]{1,0:T(8,128)} %log_add_fusion.2, pred[256,1024]{1,0:T(8,128)(4,1)} %copy-done.5), kind=kOutput, calls=%fused_computation.50.clone.1 | convolution fusion | flops 438046720 | bytes 27406336 | tf_op jit(solution)/shard_map/while/body/eval_jaxpr/hqk,qhd->khd/dot_general | solution.py:218
  369.1 34.5 %fusion.225 = f32[256,12,64]{0,2,1:T(8,128)} fusion(bf16[1024,12,64]{0,2,1:T(8,128)(2,1)} %bitcast.194, f32[12,256,1024]{2,1,0:T(8,128)} %fusion.223, f32[12,256,1024]{2,1,0:T(8,128)} %copy-done, f32[12,256]{1,0:T(8,128)S(1)} %copy-done.32, pred[256,1024]{1,0:T(8,128)(4,1)S(1)} %copy-done.6), kind=kOutput, calls=%fused_computation.51.clone.1 | convolution fusion | flops 437260288 | bytes 27799552 | tf_op jit(solution)/shard_map/while/body/eval_jaxpr/hqk,khd->qhd/dot_general | solution.py:212
  403.6 7.8 fusion.226
  454.5 40.3 %all-reduce.27 = (bf16[2304]{0:T(1024)(128)(2,1)S(1)}, bf16[3072]{0:T(1024)(128)(2,1)S(1)}, bf16[768]{0:T(1024)(128)(2,1)S(1)}, bf16[768]{0:T(1024)(128)(2,1)S(1...) all-reduce(bf16[2304]{0:T(1024)(128)(2,1)S(1)} %dynamic-update-slic, ...), channel_id=1, replica_groups=mesh['dp'=8,'seq'=4] {'dp','seq'}, use_global_device_ids=true, to_apply=%add | all-reduce | flops 9984 | bytes 39936 | tf_op jit(solution)/shard_map/while
  494.8 16.2 %all-gather.7.cloned.1.call-done = bf16[768,2304]{1,0:T(8,128)(2,1)} async-done(((bf16[24,2304]{1,0:T(8,128)(2,1)}), bf16[768,2304]{1,0:T(8,128)(2,1)}) %all-gather.7.cloned.1.call-update) | async-done | bytes 3538960 | tf_op jit(solution)/shard_map/while/body/eval_jaxpr/all_gather | solution.py:63
  536.8 19.7 %all-gather.11.cloned.1.call-done = bf16[1024,768]{0,1:T(8,128)(2,1)} async-done(((bf16[256,768]{0,1:T(8,128)(2,1)}), bf16[1024,768]{0,1:T(8,128)(2,1)}) %all-gather.11.cloned.1.call-update) | async-done | bytes 1572880 | tf_op jit(solution)/shard_map/while/body/eval_jaxpr/all_gather | solution.py:97
  568.7 44.7 %all-gather.13.cloned.1.call-done = bf16[768,768]{1,0:T(8,128)(2,1)} async-done(((bf16[24,768]{1,0:T(8,128)(2,1)}), bf16[768,768]{1,0:T(8,128)(2,1)}) %all-gather.13.cloned.1.call-update) | async-done | bytes 1179664 | tf_op jit(solution)/shard_map/while/body/eval_jaxpr/all_gather | solution.py:65
  616.2 62.7 %all-gather.15.cloned.1.call-done = bf16[768,3072]{1,0:T(8,128)(2,1)} async-done(((bf16[24,3072]{1,0:T(8,128)(2,1)}), bf16[768,3072]{1,0:T(8,128)(2,1)}) %all-gather.15.cloned.1.call-update) | async-done | bytes 4718608 | tf_op jit(solution)/shard_map/while/body/eval_jaxpr/all_gather | solution.py:74
  678.9 12.0 multiply_convert_fusion.3
  690.9 53.3 %all-gather.17.cloned.1.call-done = bf16[3072,768]{1,0:T(8,128)(2,1)} async-done(((bf16[96,768]{1,0:T(8,128)(2,1)}), bf16[3072,768]{1,0:T(8,128)(2,1)}) %all-gather.17.cloned.1.call-update) | async-done | bytes 4718608 | tf_op jit(solution)/shard_map/while/body/eval_jaxpr/all_gather | solution.py:76
  761.2 7.3 fusion.223
  768.6 35.0 %fusion.224 = bf16[12,64,1024]{2,1,0:T(8,128)(2,1)} fusion(bf16[256,12,64]{0,2,1:T(8,128)(2,1)} %copy-done.16, f32[12,256,1024]{2,1,0:T(8,128)} %fusion.223, f32[12,256,1024]{2,1,0:T(8,128)} %copy-done, f32[12,256]{1,0:T(8,128)} %log_add_fusion.2, pred[256,1024]{1,0:T(8,128)(4,1)} %copy-done.5), kind=kOutput, calls=%fused_computation.50.clone.1 | convolution fusion | flops 438046720 | bytes 27406336 | tf_op jit(solution)/shard_map/while/body/eval_jaxpr/hqk,qhd->khd/dot_general | solution.py:218
  805.7 34.5 %fusion.225 = f32[256,12,64]{0,2,1:T(8,128)} fusion(bf16[1024,12,64]{0,2,1:T(8,128)(2,1)} %bitcast.194, f32[12,256,1024]{2,1,0:T(8,128)} %fusion.223, f32[12,256,1024]{2,1,0:T(8,128)} %copy-done, f32[12,256]{1,0:T(8,128)S(1)} %copy-done.32, pred[256,1024]{1,0:T(8,128)(4,1)S(1)} %copy-done.6), kind=kOutput, calls=%fused_computation.51.clone.1 | convolution fusion | flops 437260288 | bytes 27799552 | tf_op jit(solution)/shard_map/while/body/eval_jaxpr/hqk,khd->qhd/dot_general | solution.py:212
  840.2 7.8 fusion.226
  857.4 8.9 select_add_fusion.29
  866.3 8.9 select_add_fusion.27
  882.6 7.2 select_add_fusion.22
  897.0 40.5 %all-reduce.25 = (f32[2304]{0:T(1024)S(1)}, f32[768]{0:T(1024)S(1)}, f32[768]{0:T(1024)S(1)}, f32[768]{0:T(1024)S(1)}, f32[3072]{0:T(1024)S(1)}, /*index=5*/f32[...) all-reduce(f32[2304]{0:T(1024)S(1)} %copy-done.26, ...), channel_id=5, replica_groups=mesh['dp'=8,'seq'=4] {'dp','seq'}, use_global_device_ids=true, to_apply=%region_26.27.clone | all-reduce | flops 9984 | bytes 79872
  942.2 56.3 %reduce-scatter.9.cloned.1.call-done = f32[24,768]{1,0:T(8,128)} async-done(((f32[768,768]{1,0:T(8,128)}), f32[24,768]{1,0:T(8,128)}) %reduce-scatter.9.cloned.1.call-update) | async-done | bytes 73744 | tf_op jit(solution)/shard_map/reduce_scatter | solution.py:305
  998.5 125.0 %reduce-scatter.7.cloned.1.call-done = f32[24,2304]{1,0:T(8,128)} async-done(((f32[768,2304]{1,0:T(8,128)}), f32[24,2304]{1,0:T(8,128)}) %reduce-scatter.7.cloned.1.call-update) | async-done | bytes 221200 | tf_op jit(solution)/shard_map/reduce_scatter | solution.py:303
  1123.5 141.1 %reduce-scatter.11.cloned.1.call-done = f32[24,3072]{1,0:T(8,128)} async-done(((f32[768,3072]{1,0:T(8,128)}), f32[24,3072]{1,0:T(8,128)}) %reduce-scatter.11.cloned.1.call-update) | async-done | bytes 294928 | tf_op jit(solution)/shard_map/reduce_scatter | solution.py:309
  1264.6 142.0 %reduce-scatter.13.cloned.1.call-done = f32[96,768]{1,0:T(8,128)} async-done(((f32[3072,768]{1,0:T(8,128)}), f32[96,768]{1,0:T(8,128)}) %reduce-scatter.13.cloned.1.call-update) | async-done | bytes 294928 | tf_op jit(solution)/shard_map/reduce_scatter | solution.py:311
  (508 shorter events, 187.3 us)
Async XLA Ops:
  8.6 66.6 %all-gather.7.cloned.1.call-start = ((), (), s32[]{:S(2)}) async-start(), calls=%async_computation.10 | async-start | bytes 3649536 | tf_op jit(solution)/shard_map/while/body/eval_jaxpr/all_gather | solution.py:63
  9.3 90.0 %all-gather.9.cloned.1.call-start = ((), (), s32[]{:S(2)}) async-start(), calls=%async_computation.11 | async-start | bytes 1966080 | tf_op jit(solution)/shard_map/while/body/eval_jaxpr/all_gather | solution.py:98
  80.6 40.1 %all-gather.11.cloned.1.call-start = ((), (), s32[]{:S(2)}) async-start(), calls=%async_computation.12 | async-start | bytes 1966080 | tf_op jit(solution)/shard_map/while/body/eval_jaxpr/all_gather | solution.py:97
  89.3 88.3 %all-gather.13.cloned.1.call-start = ((), (), s32[]{:S(2)}) async-start(), calls=%async_computation.13 | async-start | bytes 1216512 | tf_op jit(solution)/shard_map/while/body/eval_jaxpr/all_gather | solution.py:65
  89.9 153.1 %all-gather.15.cloned.1.call-start = ((), (), s32[]{:S(2)}) async-start(), calls=%async_computation.14 | async-start | bytes 4866048 | tf_op jit(solution)/shard_map/while/body/eval_jaxpr/all_gather | solution.py:74
  90.5 217.7 %all-gather.17.cloned.1.call-start = ((), (), s32[]{:S(2)}) async-start(), calls=%async_computation.15 | async-start | bytes 4866048 | tf_op jit(solution)/shard_map/while/body/eval_jaxpr/all_gather | solution.py:76
  91.0 337.4 %reduce-scatter.15.cloned.1.call-start = ((), (), s32[]{:S(2)}) async-start(), calls=%async_computation.16 | async-start | bytes 1966080 | tf_op jit(solution)/shard_map/while/body/eval_jaxpr/reduce_scatter | solution.py:222
  91.7 36.5 %copy-start.5 = (pred[256,1024]{1,0:T(8,128)(4,1)}, pred[256,1024]{1,0:T(8,128)(4,1)S(1)}, u32[]{:S(2)}) copy-start(pred[256,1024]{1,0:T(8,128)(4,1)S(1)} %broadcast_compare_fusion.2) | copy-start | bytes 786436 | tf_op jit(solution)/shard_map/while
  132.9 122.0 %copy-start.14 = (bf16[12,64,256]{2,1,0:T(8,128)(2,1)}, bf16[12,64,256]{2,1,0:T(8,128)(2,1)S(1)}, u32[]{:S(2)}) copy-start(bf16[12,64,256]{2,1,0:T(8,128)(2,1)S(1)} %fusion.215) | copy-start | bytes 1179652 | tf_op jit(solution)/shard_map/while
  179.8 140.3 %copy-start.27 = (f32[256]{0:T(256)}, f32[256]{0:T(256)S(1)}, u32[]{:S(2)}) copy-start(f32[256]{0:T(256)S(1)} %fusion.217) | copy-start | bytes 3076 | tf_op jit(solution)/shard_map/while
  332.6 35.8 %copy-start.34 = (f32[3072]{0:T(1024)S(1)}, f32[3072]{0:T(1024)}, u32[]{:S(2)}) copy-start(f32[3072]{0:T(1024)} %get-tuple-element.971) | copy-start | bytes 36868 | tf_op jit(solution)/shard_map/while
  332.6 36.4 %copy-start.6 = (pred[256,1024]{1,0:T(8,128)(4,1)S(1)}, pred[256,1024]{1,0:T(8,128)(4,1)}, u32[]{:S(2)}) copy-start(pred[256,1024]{1,0:T(8,128)(4,1)} %copy-done.5) | copy-start | bytes 786436 | tf_op jit(solution)/shard_map/while
  332.6 36.4 %copy-start.32 = (f32[12,256]{1,0:T(8,128)S(1)}, f32[12,256]{1,0:T(8,128)}, u32[]{:S(2)}) copy-start(f32[12,256]{1,0:T(8,128)} %log_add_fusion.2) | copy-start | bytes 36868 | tf_op jit(solution)/shard_map/while
  367.6 71.0 %reduce-scatter.17.cloned.1.call-start = ((), (), s32[]{:S(2)}) async-start(), calls=%async_computation.17 | async-start | bytes 1966080 | tf_op jit(solution)/shard_map/while/body/eval_jaxpr/reduce_scatter | solution.py:225
  447.0 64.0 %all-gather.7.cloned.1.call-start = ((), (), s32[]{:S(2)}) async-start(), calls=%async_computation.10 | async-start | bytes 3649536 | tf_op jit(solution)/shard_map/while/body/eval_jaxpr/all_gather | solution.py:63
  447.7 87.4 %all-gather.9.cloned.1.call-start = ((), (), s32[]{:S(2)}) async-start(), calls=%async_computation.11 | async-start | bytes 1966080 | tf_op jit(solution)/shard_map/while/body/eval_jaxpr/all_gather | solution.py:98
  516.4 40.1 %all-gather.11.cloned.1.call-start = ((), (), s32[]{:S(2)}) async-start(), calls=%async_computation.12 | async-start | bytes 1966080 | tf_op jit(solution)/shard_map/while/body/eval_jaxpr/all_gather | solution.py:97
  525.1 88.3 %all-gather.13.cloned.1.call-start = ((), (), s32[]{:S(2)}) async-start(), calls=%async_computation.13 | async-start | bytes 1216512 | tf_op jit(solution)/shard_map/while/body/eval_jaxpr/all_gather | solution.py:65
  525.7 153.2 %all-gather.15.cloned.1.call-start = ((), (), s32[]{:S(2)}) async-start(), calls=%async_computation.14 | async-start | bytes 4866048 | tf_op jit(solution)/shard_map/while/body/eval_jaxpr/all_gather | solution.py:74
  526.4 217.7 %all-gather.17.cloned.1.call-start = ((), (), s32[]{:S(2)}) async-start(), calls=%async_computation.15 | async-start | bytes 4866048 | tf_op jit(solution)/shard_map/while/body/eval_jaxpr/all_gather | solution.py:76
  527.0 348.3 %reduce-scatter.15.cloned.1.call-start = ((), (), s32[]{:S(2)}) async-start(), calls=%async_computation.16 | async-start | bytes 1966080 | tf_op jit(solution)/shard_map/while/body/eval_jaxpr/reduce_scatter | solution.py:222
  527.6 36.3 %copy-start.5 = (pred[256,1024]{1,0:T(8,128)(4,1)}, pred[256,1024]{1,0:T(8,128)(4,1)S(1)}, u32[]{:S(2)}) copy-start(pred[256,1024]{1,0:T(8,128)(4,1)S(1)} %broadcast_compare_fusion.2) | copy-start | bytes 786436 | tf_op jit(solution)/shard_map/while
  568.7 122.2 %copy-start.14 = (bf16[12,64,256]{2,1,0:T(8,128)(2,1)}, bf16[12,64,256]{2,1,0:T(8,128)(2,1)S(1)}, u32[]{:S(2)}) copy-start(bf16[12,64,256]{2,1,0:T(8,128)(2,1)S(1)} %fusion.215) | copy-start | bytes 1179652 | tf_op jit(solution)/shard_map/while
  615.5 140.5 %copy-start.27 = (f32[256]{0:T(256)}, f32[256]{0:T(256)S(1)}, u32[]{:S(2)}) copy-start(f32[256]{0:T(256)S(1)} %fusion.217) | copy-start | bytes 3076 | tf_op jit(solution)/shard_map/while
  768.5 35.8 %copy-start.34 = (f32[3072]{0:T(1024)S(1)}, f32[3072]{0:T(1024)}, u32[]{:S(2)}) copy-start(f32[3072]{0:T(1024)} %get-tuple-element.971) | copy-start | bytes 36868 | tf_op jit(solution)/shard_map/while
  768.5 37.1 %copy-start.6 = (pred[256,1024]{1,0:T(8,128)(4,1)S(1)}, pred[256,1024]{1,0:T(8,128)(4,1)}, u32[]{:S(2)}) copy-start(pred[256,1024]{1,0:T(8,128)(4,1)} %copy-done.5) | copy-start | bytes 786436 | tf_op jit(solution)/shard_map/while
  768.5 37.1 %copy-start.32 = (f32[12,256]{1,0:T(8,128)S(1)}, f32[12,256]{1,0:T(8,128)}, u32[]{:S(2)}) copy-start(f32[12,256]{1,0:T(8,128)} %log_add_fusion.2) | copy-start | bytes 36868 | tf_op jit(solution)/shard_map/while
  803.6 77.6 %reduce-scatter.17.cloned.1.call-start = ((), (), s32[]{:S(2)}) async-start(), calls=%async_computation.17 | async-start | bytes 1966080 | tf_op jit(solution)/shard_map/while/body/eval_jaxpr/reduce_scatter | solution.py:225
  894.4 104.1 %reduce-scatter.9.cloned.1.call-start = ((), (), s32[]{:S(2)}) async-start(), calls=%async_computation.7 | async-start | bytes 2433024 | tf_op jit(solution)/shard_map/reduce_scatter | solution.py:305
  895.0 228.5 %reduce-scatter.7.cloned.1.call-start = ((), (), s32[]{:S(2)}) async-start(), calls=%async_computation.6 | async-start | bytes 7299072 | tf_op jit(solution)/shard_map/reduce_scatter | solution.py:303
  895.6 369.0 %reduce-scatter.11.cloned.1.call-start = ((), (), s32[]{:S(2)}) async-start(), calls=%async_computation.8 | async-start | bytes 9732096 | tf_op jit(solution)/shard_map/reduce_scatter | solution.py:309
  896.2 510.4 %reduce-scatter.13.cloned.1.call-start = ((), (), s32[]{:S(2)}) async-start(), calls=%async_computation.9 | async-start | bytes 9732096 | tf_op jit(solution)/shard_map/reduce_scatter | solution.py:311
  (110 other events, 867.0 us)
Sparse Core Ops, SparseCore 0:
  12.3 62.8 all-gather.6
  80.8 18.5 all-gather.8
  100.9 19.8 all-gather.10
  123.5 54.0 all-gather.12
  180.3 62.5 all-gather.14
  245.7 62.4 all-gather.16
  367.8 26.9 reduce-scatter.14
  411.6 26.9 reduce-scatter.16
  450.7 60.2 all-gather.6
  516.5 18.5 all-gather.8
  536.7 19.8 all-gather.10
  559.3 54.0 all-gather.12
  616.3 62.5 all-gather.14
  681.6 62.4 all-gather.16
  803.7 26.9 reduce-scatter.14
  848.2 26.9 reduce-scatter.16
Sparse Core Ops, SparseCore 1:
  900.8 97.7 reduce-scatter.8
  1005.6 117.8 reduce-scatter.6
  1129.8 134.7 reduce-scatter.10
  1272.1 134.5 reduce-scatter.12
where the time goes:
time: 1420 us; the launch traced here: 1410 us
  waiting for transfers between devices  881 us (62%)
  matrix products  288 us (20%)
  blocking collectives  124 us (9%)
  local copies, waits for them, and re-layouts  54.5 us (4%)
  other arithmetic  44.5 us (3%)
  between operations  16 us (1%)
    reduce_scatter x1, waiting for transfers between devices, on_device(): lax.psum_scatter(running[8], ('dp', 'seq'), scatter_dimension=0, tiled=True)  142 us
    reduce_scatter x1, waiting for transfers between devices, on_device(): lax.psum_scatter(running[6], ('dp', 'seq'), scatter_dimension=0, tiled=True)  141 us
    all_gather x2, waiting for transfers between devices, fetch_feed(): lax.all_gather(local_set[0], ('dp', 'seq'), axis=0, tiled=True)  125 us
    reduce_scatter x1, waiting for transfers between devices, on_device(): lax.psum_scatter(running[0], ('dp', 'seq'), scatter_dimension=0, tiled=True)  125 us
    all_gather x2, waiting for transfers between devices, fetch_feed(): lax.all_gather(local_set[2], ('dp', 'seq'), axis=0, tiled=True)  106 us
    all_gather x2, waiting for transfers between devices, fetch_attention(): lax.all_gather(local_set[2], ('dp', 'seq'), axis=0, tiled=True)  89.3 us
    while x2, blocking collectives  83.2 us
    dot_general x2, matrix products, backward_pass(): jnp.einsum('hqk,qhd->khd', d_scores, query_heads, preferred_element_type=...  70 us
  transfers between devices with their start and end apart: 20, of which 17 were waited for; matrix products, arithmetic and copies ran while one was open for 17% of the time, Pallas kernels for 0%

commit v1 on v0

v1 whole, which is shorter than its diff:
```python
import jax
import jax.numpy as jnp
from jax import lax
from jax.sharding import PartitionSpec as P

D = 768
HEADS = 12
HD = 64
FF = 3072
EPSILON = 1e-06
ALL = ("dp", "seq")
BF = jnp.bfloat16
F32 = jnp.float32
SMALL = (3 * D, D, D, D, FF, D, D, D)


def mm(a, b):
    return jnp.dot(a, b, preferred_element_type=F32)


def layer_norm(values, gain_vec, shift_vec):
    center = values - jnp.mean(values, axis=-1, keepdims=True)
    spread = jnp.mean(center * center, axis=-1, keepdims=True)
    return center * lax.rsqrt(spread + EPSILON) * gain_vec + shift_vec


def gelu_exact(values):
    return jax.nn.gelu(values, approximate=False)


def rotary_tables(segments, offset, row_count):
    length = segments.shape[-1]
    places = jnp.arange(length, dtype=jnp.int32)[None]
    change = jnp.concatenate(
        [jnp.ones((segments.shape[0], 1), dtype=bool), segments[:, 1:] != segments[:, :-1]], axis=1
    )
    starts = lax.cummax(jnp.where(change, places, 0), axis=1)
    position = lax.dynamic_slice_in_dim(places - starts, offset, row_count, 1).astype(F32)
    inverse = 10000.0 ** (-2.0 * jnp.arange(HD // 2, dtype=F32) / HD)
    angles = position[..., None] * inverse
    return jnp.cos(angles), jnp.sin(angles)


def rotate(values, cos_part, sin_part):
    paired = values.reshape(values.shape[:-1] + (HEADS, HD // 2, 2))
    even, odd = paired[..., 0], paired[..., 1]
    cos_wide, sin_wide = cos_part[..., None, :], sin_part[..., None, :]
    turned = jnp.stack(
        [even * cos_wide - odd * sin_wide, even * sin_wide + odd * cos_wide], axis=-1
    )
    return turned.reshape(values.shape)


def gather(local):
    return lax.all_gather(local, ALL, axis=0, tiled=True)


def gather_small(parts):
    joined = gather(jnp.concatenate(parts)[None])
    out, at = [], 0
    for part in parts:
        n = part.shape[0]
        out.append(joined[:, at : at + n].reshape(-1))
        at += n
    return out


def scatter_small(sums, devices):
    joined = jnp.concatenate([s.reshape(devices, -1) for s in sums], axis=1)
    own = lax.psum_scatter(joined, ALL, scatter_dimension=0, tiled=True)[0]
    out, at = [], 0
    for s in sums:
        n = s.shape[0] // devices
        out.append(own[at : at + n])
        at += n
    return out


def scatter(grad):
    return lax.psum_scatter(grad.astype(BF), ALL, scatter_dimension=0, tiled=True).astype(F32)


def heads(values):
    return values.reshape(values.shape[0], values.shape[1], HEADS, HD)


def scores_of(query, key_all, same_doc):
    raw = jnp.einsum("bqhd,bkhd->bhqk", heads(query), heads(key_all), preferred_element_type=F32)
    return jnp.where(same_doc[:, None], raw * HD ** (-0.5), -1e30)


def on_device(devices, *args):
    (tokens, segment_ids, w_qkv, b_qkv, w_out, b_out, gain_one, shift_one) = args[:8]
    (w_in, b_in, w_back, b_back, gain_two, shift_two, out_grad) = args[8:]
    b_qkv, b_out, gain_one, shift_one, b_in, b_back, gain_two, shift_two = [
        v.astype(F32)
        for v in gather_small([b_qkv, b_out, gain_one, shift_one, b_in, b_back, gain_two, shift_two])
    ]
    w_qkv, w_out, w_in, w_back = gather(w_qkv), gather(w_out), gather(w_in), gather(w_back)
    batch, rows = tokens.shape[:2]
    flat = (batch * rows, D)
    offset = lax.axis_index("seq") * rows
    cos_part, sin_part = rotary_tables(segment_ids, offset, rows)
    own_ids = lax.dynamic_slice_in_dim(segment_ids, offset, rows, 1)
    same_doc = own_ids[:, :, None] == segment_ids[:, None, :]

    tok = tokens.reshape(flat)
    joined = (mm(tok, w_qkv) + b_qkv).reshape(batch, rows, 3 * D)
    query = rotate(joined[..., :D], cos_part, sin_part).astype(BF)
    key = rotate(joined[..., D : 2 * D], cos_part, sin_part).astype(BF)
    value = joined[..., 2 * D :].astype(BF)
    key_all = lax.all_gather(key, "seq", axis=1, tiled=True)
    value_all = lax.all_gather(value, "seq", axis=1, tiled=True)
    keys = key_all.shape[1]
    scores = scores_of(query, key_all, same_doc)
    highest = jnp.max(scores, axis=-1, keepdims=True)
    exponent = jnp.exp(scores - highest)
    total = jnp.sum(exponent, axis=-1, keepdims=True)
    log_total = highest + jnp.log(total)
    mixed = jnp.einsum(
        "bhqk,bkhd->bqhd", (exponent / total).astype(BF), heads(value_all),
        preferred_element_type=F32,
    ).astype(BF).reshape(flat)
    first_sum = tok.astype(F32) + mm(mixed, w_out) + b_out
    normed = layer_norm(first_sum, gain_one, shift_one)
    normed_low = normed.astype(BF)
    inner = mm(normed_low, w_in) + b_in
    active = gelu_exact(inner).astype(BF)
    second_sum = normed + mm(active, w_back) + b_back
    result, pull_two = jax.vjp(layer_norm, second_sum, gain_two, shift_two)
    layer_out = result.astype(BF).reshape(tokens.shape)

    d_second_sum, d_gain_two, d_shift_two = pull_two(out_grad.reshape(flat).astype(F32))
    d_second = d_second_sum.astype(BF)
    d_b_back = jnp.sum(d_second.astype(F32), axis=0)
    d_w_back = scatter(jnp.einsum("qf,qd->fd", active, d_second, preferred_element_type=F32))
    d_active = jnp.einsum("qd,fd->qf", d_second, w_back, preferred_element_type=F32)
    d_inner = jax.vjp(gelu_exact, inner)[1](d_active)[0].astype(BF)
    d_b_in = jnp.sum(d_inner.astype(F32), axis=0)
    d_w_in = scatter(jnp.einsum("qd,qf->df", normed_low, d_inner, preferred_element_type=F32))
    d_normed = d_second_sum + jnp.einsum("qf,df->qd", d_inner, w_in, preferred_element_type=F32)
    d_first_sum, d_gain_one, d_shift_one = jax.vjp(layer_norm, first_sum, gain_one, shift_one)[1](
        d_normed
    )
    d_branch = d_first_sum.astype(BF)
    d_b_out = jnp.sum(d_branch.astype(F32), axis=0)
    d_w_out = scatter(jnp.einsum("qd,qe->de", mixed, d_branch, preferred_element_type=F32))
    d_mixed = jnp.einsum("qe,de->qd", d_branch, w_out, preferred_element_type=F32).astype(BF)
    d_mixed = d_mixed.reshape(batch, rows, D)

    attention = jnp.exp(scores_of(query, key_all, same_doc) - log_total)
    d_attention = jnp.einsum(
        "bqhd,bkhd->bhqk", heads(d_mixed), heads(value_all), preferred_element_type=F32
    )
    inner_sum = jnp.sum(d_attention * attention, axis=-1, keepdims=True)
    d_scores = (attention * (d_attention - inner_sum) * HD ** (-0.5)).astype(BF)
    d_query = jnp.einsum(
        "bhqk,bkhd->bqhd", d_scores, heads(key_all), preferred_element_type=F32
    ).reshape(batch, rows, D)
    d_value = jnp.einsum(
        "bhqk,bqhd->bkhd", attention.astype(BF), heads(d_mixed), preferred_element_type=F32
    ).reshape(batch, keys, D)
    d_key = jnp.einsum(
        "bhqk,bqhd->bkhd", d_scores, heads(query), preferred_element_type=F32
    ).reshape(batch, keys, D)
    d_key = lax.psum_scatter(d_key.astype(BF), "seq", scatter_dimension=1, tiled=True).astype(F32)
    d_value = lax.psum_scatter(d_value.astype(BF), "seq", scatter_dimension=1, tiled=True)
    d_joined = jnp.concatenate(
        [
            rotate(d_query, cos_part, -sin_part).astype(BF),
            rotate(d_key, cos_part, -sin_part).astype(BF),
            d_value,
        ],
        axis=-1,
    ).reshape(batch * rows, 3 * D)
    d_b_qkv = jnp.sum(d_joined.astype(F32), axis=0)
    d_w_qkv = scatter(jnp.einsum("qd,qe->de", tok, d_joined, preferred_element_type=F32))
    d_tokens = (
        jnp.einsum("qe,de->qd", d_joined, w_qkv, preferred_element_type=F32) + d_first_sum
    ).reshape(tokens.shape)
    small = scatter_small(
        [d_b_qkv, d_b_out, d_gain_one, d_shift_one, d_b_in, d_b_back, d_gain_two, d_shift_two],
        devices,
    )
    return (
        layer_out, d_tokens, d_w_qkv, small[0], d_w_out, small[1], small[2], small[3],
        d_w_in, small[4], d_w_back, small[5], small[6], small[7],
    )


def solution(mesh):
    devices = mesh.shape["dp"] * mesh.shape["seq"]
    rows3 = P("dp", "seq", None)
    mat, vec = P(ALL, None), P(ALL)
    params = (mat, vec, mat, vec, vec, vec, mat, vec, mat, vec, vec, vec)
    return jax.shard_map(
        lambda *args: on_device(devices, *args),
        mesh=mesh,
        in_specs=(rows3, P("dp", None)) + params + (rows3,),
        out_specs=(rows3, rows3) + params,
        check_vma=False,
    )
```

time: 1420 us -> 961 us (0.68)
  waiting for transfers between devices: 881 us -> 535 us
  matrix products: 288 us -> 233 us
  blocking collectives: 124 us -> 82.8 us
    all_gather x12 -> x6, waiting for transfers between devices: 406 us -> 183 us  [the longest x4 159 us: gather(): return lax.all_gather(local, ALL, axis=0, tiled=True)]
    reduce_scatter x8 -> x5, waiting for transfers between devices: 469 us -> 292 us  [the longest x3 292 us: scatter(): lax.psum_scatter(grad.astype(BF), ALL, scatter_dimension=0, tiled=True)]
    while x2 -> x0, blocking collectives: 83.2 us -> none
    unnamed x4 -> x13, waiting for transfers between devices: 2.19 us -> 59.7 us
    dot_general x36 -> x18, matrix products: 288 us -> 233 us  [the longest x1 53.5 us: on_device(): jnp.einsum('bhqk,bqhd->bkhd', d_scores, heads(query), preferred_element_t...]
    unnamed x1 -> x2, blocking collectives: 40.5 us -> 82.8 us
    while x268 -> x0, local copies, waits for them, and re-layouts: 23.6 us -> none
  transfers between devices with their start and end apart: 20 -> 12, of which waited for: 17 -> 10; matrix products, arithmetic and copies ran while one was open for 17% -> 21% of each run, Pallas kernels for 0% -> 0%
where the time goes in v1:
time: 961 us; the launch traced here: 954 us
  waiting for transfers between devices  535 us (56%)
  matrix products  233 us (24%)
  blocking collectives  82.8 us (9%)
  local copies, waits for them, and re-layouts  53 us (6%)
  other arithmetic  34.1 us (4%)
  between operations  15.2 us (2%)
    reduce_scatter x3, waiting for transfers between devices, scatter(): lax.psum_scatter(grad.astype(BF), ALL, scatter_dimension=0, tiled=True)  292 us
    all_gather x4, waiting for transfers between devices, gather(): return lax.all_gather(local, ALL, axis=0, tiled=True)  159 us
    unnamed x2, blocking collectives  82.8 us
    unnamed x13, waiting for transfers between devices  59.7 us
    dot_general x1, matrix products, on_device(): jnp.einsum('bhqk,bqhd->bkhd', d_scores, heads(query), preferred_element_t...  53.5 us
    dot_general x1, matrix products, on_device(): jnp.einsum('bhqk,bkhd->bqhd', d_scores, heads(key_all), preferred_element...  51.8 us
    dot_general x4, matrix products, mm(): return jnp.dot(a, b, preferred_element_type=F32)  34.4 us
  transfers between devices with their start and end apart: 12, of which 10 were waited for; matrix products, arithmetic and copies ran while one was open for 21% of the time, Pallas kernels for 0%

profile of v1, /device:TPU:0, one launch (start us, length us, event | category | flops | bytes accessed | tf_op | source)
XLA Modules:
  0.0 953.9 jit_solution(14345819672077797248)
XLA Ops:
  10.0 5.4 concatenate.12
  15.7 42.4 %all-reduce.1 = bf16[9984]{0:T(1024)(128)(2,1)S(1)} all-reduce(bf16[9984]{0:T(1024)(128)(2,1)S(1)} %dynamic-update-slice), channel_id=2, replica_groups=mesh['dp'=8,'seq'=4] {'dp','seq'}, use_global_device_ids=true, to_apply=%add.1 | all-reduce | flops 9984 | bytes 39936
  60.1 13.7 %all-gather.8.cloned.1.call-done = bf16[768,2304]{1,0:T(8,128)(2,1)} async-done(((bf16[24,2304]{1,0:T(8,128)(2,1)}), bf16[768,2304]{1,0:T(8,128)(2,1)}) %all-gather.8.cloned.1.call-update) | async-done | bytes 3538960 | tf_op jit(solution)/shard_map/all_gather | solution.py:55
  73.8 4.3 convolution_add_fusion
  84.1 3.1 subtract_convert_fusion.3
  98.8 18.3 %all-gather.12.cloned.1.call-done = bf16[2,1024,768]{1,2,0:T(8,128)(2,1)} async-done(((bf16[2,256,768]{1,2,0:T(8,128)(2,1)}), bf16[2,1024,768]{1,2,0:T(8,128)(2,1)}) %all-gather.12.cloned.1.call-update) | async-done | bytes 3145744 | tf_op jit(solution)/shard_map/all_gather | solution.py:112
  117.2 13.2 %fusion.3 = (f32[2,12,256]{2,1,0:T(8,128)S(1)}, f32[2,12,256,1024]{3,2,1,0:T(8,128)}) fusion(pred[2,256,1024]{2,1,0:T(8,128)(4,1)S(1)} %broadcast_compare_fusion, bf16[2,1024,12,64]{1,3,2,0:T(8,128)(2,1)} %bitcast.120, bf16[2,256,12,64]{1,0,3,2:T(2,128)(2,1)S(1)} %bitcast.122), kind=kOutput, calls=%fused_computation.9 | convolution fusion | flops 824174592 | bytes 29646848 | tf_op jit(solution)/shard_map/bqhd,bkhd->bhqk/dot_general | solution.py:88
  130.4 11.8 %fusion.2 = f32[2,12,256]{2,1,0:T(8,128)S(1)} fusion(f32[2,12,256,1024]{3,2,1,0:T(8,128)} %get-tuple-element.104, f32[2,12,256]{2,1,0:T(8,128)S(1)} %get-tuple-element.103, pred[2,256,1024]{2,1,0:T(8,128)(4,1)S(1)} %broadcast_compare_fusion), kind=kLoop, calls=%fused_computation.8 | loop fusion | flops 25159680 | bytes 25739264 | tf_op jit(solution)/shard_map/reduce_sum | solution.py:118
  142.2 5.7 all-gather.10.cloned.1.call-done
  147.9 3.2 copy.53
  151.1 11.7 %fusion.36 = bf16[2,256,12,64]{1,3,2,0:T(8,128)(2,1)S(1)} fusion(bf16[2,1024,12,64]{1,3,2,0:T(8,128)(2,1)S(1)} %bitcast.106, f32[2,12,256,1024]{3,2,1,0:T(8,128)} %get-tuple-element.104, f32[2,12,256]{2,1,0:T(8,128)S(1)} %fusion.2, f32[2,12,256]{2,1,0:T(8,128)S(1)} %get-tuple-element.103, pred[2,256,1024]{2,1,0:T(8,128)(4,1)} %copy-done.7), kind=kOutput, calls=%fused_computation.69 | convolution fusion | flops 837156864 | bytes 29671424 | tf_op jit(solution)/shard_map/bhqk,bkhd->bqhd/dot_general | solution.py:120
  164.7 40.0 %all-gather.14.cloned.1.call-done = bf16[768,768]{1,0:T(8,128)(2,1)} async-done(((bf16[24,768]{1,0:T(8,128)(2,1)}), bf16[768,768]{1,0:T(8,128)(2,1)}) %all-gather.14.cloned.1.call-update) | async-done | bytes 1179664 | tf_op jit(solution)/shard_map/all_gather | solution.py:55
  208.9 61.2 %all-gather.16.cloned.1.call-done = bf16[768,3072]{1,0:T(8,128)(2,1)} async-done(((bf16[24,3072]{1,0:T(8,128)(2,1)}), bf16[768,3072]{1,0:T(8,128)(2,1)}) %all-gather.16.cloned.1.call-update) | async-done | bytes 4718608 | tf_op jit(solution)/shard_map/all_gather | solution.py:55
  270.1 20.9 %multiply_convert_fusion.1 = (bf16[512,3072]{1,0:T(8,128)(2,1)}, f32[512,3072]{1,0:T(8,128)}, f32[512,3072]{1,0:T(8,128)}) fusion(f32[3072]{0:T(1024)S(1)} %copy-done.22, bf16[768,3072]{1,0:T(8,128)(2,1)} %all-gather.16.cloned.1.call-done, f32[512,768]{1,0:T(8,128)} %copy-done.3, f32[768]{0:T(1024)S(1)} %copy-done.23, f32[768]{0:T(1024)S(1)} %copy-done.21, ...), kind=kOutput, calls=%fused_computation.20 | convolution fusion | flops 2521694208 | bytes 22042624 | tf_op jit(solution)/shard_map/dot_general | solution.py:18
  291.0 44.3 %all-gather.18.cloned.1.call-done = bf16[3072,768]{1,0:T(8,128)(2,1)} async-done(((bf16[96,768]{1,0:T(8,128)(2,1)}), bf16[3072,768]{1,0:T(8,128)(2,1)}) %all-gather.18.cloned.1.call-update) | async-done | bytes 4718608 | tf_op jit(solution)/shard_map/all_gather | solution.py:55
  335.3 6.5 fusion.71
  344.9 9.6 %convert_reduce_fusion = (f32[3072]{0:T(1024)S(1)}, bf16[512,3072]{1,0:T(8,128)(2,1)}) fusion(f32[512,3072]{1,0:T(8,128)} %get-tuple-element.72, f32[512,3072]{1,0:T(8,128)} %get-tuple-element.107, f32[3072]{0:T(1024)S(1)} %copy-done.22, bf16[512,768]{1,0:T(8,128)(2,1)S(1)} %get-tuple-element.62, bf16[3072,768]{1,0:T(8,128)(2,1)S(1)} %copy-done.26), kind=kOutput, calls=%fused_computation.18 | convolution fusion | flops 2442654720 | bytes 21258240 | tf_op jit(solution)/shard_map/qd,fd->qf/dot_general | solution.py:137
  354.5 5.1 multiply_reduce_fusion.1
  369.6 11.3 %fusion.42 = f32[2,12,256,1024]{3,2,1,0:T(8,128)} fusion(bf16[2,1024,12,64]{1,3,2,0:T(8,128)(2,1)S(1)} %bitcast.107, bf16[2,256,12,64]{1,0,3,2:T(2,128)(2,1)} %reshape_reshape.7), kind=kOutput, calls=%fused_computation.90 | convolution fusion | flops 805306368 | bytes 29097984 | tf_op jit(solution)/shard_map/bqhd,bkhd->bhqk/dot_general | solution.py:152
  380.8 53.5 %fusion.22 = bf16[2,12,64,1024]{3,2,1,0:T(8,128)(2,1)} fusion(f32[2,12,256,1024]{3,2,1,0:T(8,128)} %fusion.42, f32[2,12,256]{2,1,0:T(8,128)S(1)} %log_add_fusion, f32[2,12,256,1024]{3,2,1,0:T(8,128)} %get-tuple-element.104, pred[2,256,1024]{2,1,0:T(8,128)(4,1)} %copy-done.7, bf16[2,256,12,64]{1,0,3,2:T(2,128)(2,1)} %bitcast.123), kind=kOutput, calls=%fused_computation.41 | convolution fusion | flops 876092416 | bytes 54812672 | tf_op jit(solution)/shard_map/bhqk,bqhd->bkhd/dot_general | solution.py:163
  434.4 14.5 %fusion.25 = bf16[2,12,64,1024]{3,2,1,0:T(8,128)(2,1)} fusion(f32[2,12,256]{2,1,0:T(8,128)S(1)} %log_add_fusion, f32[2,12,256,1024]{3,2,1,0:T(8,128)} %get-tuple-element.104, pred[2,256,1024]{2,1,0:T(8,128)(4,1)S(1)} %copy-done.8, bf16[2,256,12,64]{1,0,3,2:T(2,128)(2,1)S(1)} %copy-done.2), kind=kOutput, calls=%fused_computation.42 | convolution fusion | flops 832045056 | bytes 29646848 | tf_op jit(solution)/shard_map/bhqk,bqhd->bkhd/dot_general | solution.py:160
  452.1 6.5 convolution_convert_fusion.1
  459.8 6.7 convolution_convert_fusion
  466.7 51.8 %fusion.32 = f32[2,256,12,64]{1,3,2,0:T(8,128)} fusion(bf16[2,1024,12,64]{1,3,2,0:T(8,128)(2,1)} %bitcast.121, f32[2,12,256,1024]{3,2,1,0:T(8,128)} %fusion.42, f32[2,12,256]{2,1,0:T(8,128)S(1)} %log_add_fusion, f32[2,12,256,1024]{3,2,1,0:T(8,128)} %get-tuple-element.104, pred[2,256,1024]{2,1,0:T(8,128)(4,1)S(1)} %copy-done.8), kind=kOutput, calls=%fused_computation.62 | convolution fusion | flops 874519552 | bytes 55599104 | tf_op jit(solution)/shard_map/bhqk,bkhd->bqhd/dot_general | solution.py:157
  528.4 3.8 fusion.21
  532.2 5.9 copy.72
  538.9 74.4 %reduce-scatter.13.cloned.1.call-done = bf16[24,768]{1,0:T(8,128)(2,1)} async-done(((bf16[768,768]{1,0:T(8,128)(2,1)}), bf16[24,768]{1,0:T(8,128)(2,1)}) %reduce-scatter.13.cloned.1.call-update) | async-done | bytes 36880 | tf_op jit(solution)/shard_map/reduce_scatter | solution.py:80
  618.2 106.6 %reduce-scatter.15.cloned.1.call-done = bf16[24,3072]{1,0:T(8,128)(2,1)} async-done(((bf16[768,3072]{1,0:T(8,128)(2,1)}), bf16[24,3072]{1,0:T(8,128)(2,1)}) %reduce-scatter.15.cloned.1.call-update) | async-done | bytes 147472 | tf_op jit(solution)/shard_map/reduce_scatter | solution.py:80
  726.4 110.8 %reduce-scatter.17.cloned.1.call-done = bf16[96,768]{1,0:T(8,128)(2,1)} async-done(((bf16[3072,768]{1,0:T(8,128)(2,1)}), bf16[96,768]{1,0:T(8,128)(2,1)}) %reduce-scatter.17.cloned.1.call-update) | async-done | bytes 147472 | tf_op jit(solution)/shard_map/reduce_scatter | solution.py:80
  838.9 40.3 %all-reduce.2 = f32[32,312]{1,0:T(8,128)S(1)} all-reduce(f32[32,312]{1,0:T(8,128)S(1)} %concatenate.15), channel_id=6, replica_groups=mesh['dp'=8,'seq'=4] {'dp','seq'}, use_global_device_ids=true, to_apply=%region_24.25.clone | all-reduce | flops 9984 | bytes 79872
  880.9 6.3 add_add_fusion.4
  887.3 57.3 %reduce-scatter.19.cloned.1.call-done = bf16[24,2304]{1,0:T(8,128)(2,1)} async-done(((bf16[768,2304]{1,0:T(8,128)(2,1)}), bf16[24,2304]{1,0:T(8,128)(2,1)}) %reduce-scatter.19.cloned.1.call-update) | async-done | bytes 110608
  (173 shorter events, 68.4 us)
Async XLA Ops:
  7.2 66.6 %all-gather.8.cloned.1.call-start = ((), (), s32[]{:S(2)}) async-start(), calls=%async_computation.6 | async-start | bytes 3649536 | tf_op jit(solution)/shard_map/all_gather | solution.py:55
  7.9 109.3 %all-gather.12.cloned.1.call-start = ((), (), s32[]{:S(2)}) async-start(), calls=%async_computation.8 | async-start | bytes 3932160 | tf_op jit(solution)/shard_map/all_gather | solution.py:112
  58.2 19.9 %copy-start.17 = (bf16[32,312]{1,0:T(8,128)(2,1)}, bf16[32,312]{1,0:T(8,128)(2,1)S(1)}, u32[]{:S(2)}) copy-start(bf16[32,312]{1,0:T(8,128)(2,1)S(1)} %reshape.313) | copy-start | bytes 59908
  84.1 9.6 %copy-start.20 = (s32[2,1024]{1,0:T(2,128)S(1)}, s32[2,1024]{1,0:T(2,128)}, u32[]{:S(2)}) copy-start(s32[2,1024]{1,0:T(2,128)} %param.16) | copy-start | bytes 24580
  87.3 6.5 copy-start.18
  87.3 10.5 %copy-start.11 = (bf16[2,256,12,32,1]{1,0,4,3,2:T(2,128)(2,1)S(1)}, bf16[2,256,12,32,1]{1,0,4,3,2:T(2,128)(2,1)}, u32[]{:S(2)}) copy-start(bf16[2,256,12,32,1]{1,0,4,3,2:T(2,128)(2,1)} %get-tuple-element.80) | copy-start | bytes 1179652
  89.3 58.6 %all-gather.10.cloned.1.call-start = ((), (), s32[]{:S(2)}) async-start(), calls=%async_computation.7 | async-start | bytes 3932160 | tf_op jit(solution)/shard_map/all_gather | solution.py:113
  91.7 113.0 %all-gather.14.cloned.1.call-start = ((), (), s32[]{:S(2)}) async-start(), calls=%async_computation.9 | async-start | bytes 1216512 | tf_op jit(solution)/shard_map/all_gather | solution.py:55
  92.3 177.8 %all-gather.16.cloned.1.call-start = ((), (), s32[]{:S(2)}) async-start(), calls=%async_computation.10 | async-start | bytes 4866048 | tf_op jit(solution)/shard_map/all_gather | solution.py:55
  92.9 242.4 %all-gather.18.cloned.1.call-start = ((), (), s32[]{:S(2)}) async-start(), calls=%async_computation.11 | async-start | bytes 4866048 | tf_op jit(solution)/shard_map/all_gather | solution.py:55
  93.5 427.7 %reduce-scatter.9.cloned.1.call-start = ((), (), s32[]{:S(2)}) async-start(), calls=%async_computation.12 | async-start | bytes 3932160 | tf_op jit(solution)/shard_map/reduce_scatter | solution.py:166
  97.8 32.6 %copy-start.7 = (pred[2,256,1024]{2,1,0:T(8,128)(4,1)}, pred[2,256,1024]{2,1,0:T(8,128)(4,1)S(1)}, u32[]{:S(2)}) copy-start(pred[2,256,1024]{2,1,0:T(8,128)(4,1)S(1)} %broadcast_compare_fusion) | copy-start | bytes 1572868
  98.8 31.6 %copy-start.10 = (bf16[2,256,12,32,2]{1,0,4,3,2:T(2,128)(2,1)}, bf16[2,256,12,32,2]{1,0,4,3,2:T(2,128)(2,1)S(1)}, u32[]{:S(2)}) copy-start(bf16[2,256,12,32,2]{1,0,4,3,2:T(2,128)(2,1)S(1)} %pad_maximum_fusion) | copy-start | bytes 2359300
  151.1 53.6 %copy-start.25 = (f32[768]{0:T(1024)S(1)}, f32[768]{0:T(1024)}, u32[]{:S(2)}) copy-start(f32[768]{0:T(1024)} %reshape.303) | copy-start | bytes 9220
  162.8 107.3 %copy-start.21 = (f32[768]{0:T(1024)S(1)}, f32[768]{0:T(1024)}, u32[]{:S(2)}) copy-start(f32[768]{0:T(1024)} %reshape.304) | copy-start | bytes 9220
  162.8 107.2 %copy-start.22 = (f32[3072]{0:T(1024)S(1)}, f32[3072]{0:T(1024)}, u32[]{:S(2)}) copy-start(f32[3072]{0:T(1024)} %reshape.306) | copy-start | bytes 36868
  162.8 107.2 %copy-start.23 = (f32[768]{0:T(1024)S(1)}, f32[768]{0:T(1024)}, u32[]{:S(2)}) copy-start(f32[768]{0:T(1024)} %reshape.305) | copy-start | bytes 9220
  208.8 126.5 %copy-start.24 = (f32[768]{0:T(1024)S(1)}, f32[768]{0:T(1024)}, u32[]{:S(2)}) copy-start(f32[768]{0:T(1024)} %reshape.307) | copy-start | bytes 9220
  335.3 6.9 copy-start
  344.6 9.9 %slice-start = ((s8[4718592]{0:T(1024)(128)(4,1)}), s8[4194304]{0:T(1024)(128)(4,1)S(1)}, s32[]{:S(2)}) async-start(s8[4718592]{0:T(1024)(128)(4,1)} %bitcast.131), calls=%async_computation.18 | async-start | bytes 8388608
  344.8 9.6 %copy-start.13 = (bf16[512,768]{1,0:T(8,128)(2,1)}, bf16[512,768]{1,0:T(8,128)(2,1)S(1)}, u32[]{:S(2)}) copy-start(bf16[512,768]{1,0:T(8,128)(2,1)S(1)} %get-tuple-element.62) | copy-start | bytes 2359300
  344.8 9.6 %copy-start.4 = (f32[512,768]{1,0:T(8,128)S(1)}, f32[512,768]{1,0:T(8,128)}, u32[]{:S(2)}) copy-start(f32[512,768]{1,0:T(8,128)} %copy-done.3) | copy-start | bytes 4718596
  344.8 9.6 %slice-start.1 = ((s8[4718592]{0:T(1024)(128)(4,1)}), s8[524288]{0:T(1024)(128)(4,1)S(1)}, s32[]{:S(2)}) async-start(s8[4718592]{0:T(1024)(128)(4,1)} %bitcast.131), calls=%async_computation.19 | async-start | bytes 1048576
  380.8 53.6 %copy-start.2 = (bf16[2,256,12,64]{1,0,3,2:T(2,128)(2,1)S(1)}, bf16[2,256,12,64]{1,0,3,2:T(2,128)(2,1)}, u32[]{:S(2)}) copy-start(bf16[2,256,12,64]{1,0,3,2:T(2,128)(2,1)} %reshape_reshape.7) | copy-start | bytes 2359300
  380.8 53.6 %copy-start.8 = (pred[2,256,1024]{2,1,0:T(8,128)(4,1)S(1)}, pred[2,256,1024]{2,1,0:T(8,128)(4,1)}, u32[]{:S(2)}) copy-start(pred[2,256,1024]{2,1,0:T(8,128)(4,1)} %copy-done.7) | copy-start | bytes 1572868
  434.3 14.7 %copy-start.12 = (bf16[96,8,2,256]{3,1,2,0:T(8,128)(2,1)S(1)}, bf16[96,8,2,256]{3,1,2,0:T(8,128)(2,1)}, u32[]{:S(2)}) copy-start(bf16[96,8,2,256]{3,1,2,0:T(8,128)(2,1)} %copy.79) | copy-start | bytes 2359300
  434.3 92.9 %reduce-scatter.11.cloned.1.call-start = ((), (), s32[]{:S(2)}) async-start(), calls=%async_computation.13 | async-start | bytes 3932160 | tf_op jit(solution)/shard_map/reduce_scatter | solution.py:167
  448.9 164.4 %reduce-scatter.13.cloned.1.call-start = ((), (), s32[]{:S(2)}) async-start(), calls=%async_computation.14 | async-start | bytes 1216512 | tf_op jit(solution)/shard_map/reduce_scatter | solution.py:80
  452.1 272.7 %reduce-scatter.15.cloned.1.call-start = ((), (), s32[]{:S(2)}) async-start(), calls=%async_computation.15 | async-start | bytes 4866048 | tf_op jit(solution)/shard_map/reduce_scatter | solution.py:80
  458.7 378.6 %reduce-scatter.17.cloned.1.call-start = ((), (), s32[]{:S(2)}) async-start(), calls=%async_computation.16 | async-start | bytes 4866048 | tf_op jit(solution)/shard_map/reduce_scatter | solution.py:80
  466.5 478.1 %reduce-scatter.19.cloned.1.call-start = ((), (), s32[]{:S(2)}) async-start(), calls=%async_computation.17 | async-start | bytes 3649536
  532.2 5.9 copy-start.1
  (11 other events, 28.7 us)
Sparse Core Ops, SparseCore 0:
  10.9 62.8 all-gather.7
  89.4 27.7 all-gather.11
  119.3 28.5 all-gather.9
  150.6 54.0 all-gather.13
  207.5 62.5 all-gather.15
  272.8 62.4 all-gather.17
  434.4 36.7 reduce-scatter.8
  473.9 38.1 reduce-scatter.10
  517.2 96.1 reduce-scatter.12
  618.7 105.9 reduce-scatter.14
  731.1 106.0 reduce-scatter.16
  842.5 102.0 reduce-scatter.18

commit v2 on v1

--- a/solution.py
+++ b/solution.py
@@ -1,6 +1,9 @@
+import functools
 import jax
 import jax.numpy as jnp
 from jax import lax
+from jax.experimental import pallas as pl
+from jax.experimental.pallas import tpu as pltpu
 from jax.sharding import PartitionSpec as P
 
 D = 768
@@ -11,7 +14,6 @@
 ALL = ("dp", "seq")
 BF = jnp.bfloat16
 F32 = jnp.float32
-SMALL = (3 * D, D, D, D, FF, D, D, D)
 
 
 def mm(a, b):
@@ -188,13 +190,575 @@
     )
 
 
+NZ = 4
+HBM = pl.BlockSpec(memory_space=pl.ANY)
+
+
+def place():
+    dp, seq = lax.axis_index("dp"), lax.axis_index("seq")
+    return dp // 2, dp % 2, seq // 2, seq % 2
+
+
+def device(z, y, x, c):
+    return (z * 2 + y, x * 2 + c)
+
+
+def z_order(k, z):
+    low = z < 2
+    near = jnp.where(low, z, 3 - z)
+    second = {0: 1, 1: 0, 2: 2, 3: 3}[k]
+    found = jnp.where(near == 0, k, second)
+    return jnp.where(low, found, 3 - found)
+
+
+def greet():
+    z, y, x, c = place()
+    barrier = pltpu.get_barrier_semaphore()
+
+    def signal(target):
+        pl.semaphore_signal(
+            barrier, inc=1, device_id=target, device_id_type=pl.DeviceIdType.MESH
+        )
+
+    signal(device(z, y, x, 1 - c))
+    signal(device(z, y, 1 - x, c))
+    signal(device(z, 1 - y, x, c))
+    pl.when(z < NZ - 1)(lambda: signal(device(z + 1, y, x, c)))
+    pl.when(z > 0)(lambda: signal(device(z - 1, y, x, c)))
+    pl.semaphore_wait(barrier, 3 + (z < NZ - 1).astype(jnp.int32) + (z > 0).astype(jnp.int32))
+
+
+class Mail:
+    def __init__(self, send_sems, recv_sems):
+        self.send_sems, self.recv_sems = send_sems, recv_sems
+        self.sent, self.slots = [], 0
+
+    def slot(self, count):
+        at = self.slots
+        self.slots += count
+        return at
+
+    def send(self, src, dst, slot, target, cond=None):
+        copy = pltpu.make_async_remote_copy(
+            src_ref=src, dst_ref=dst, send_sem=self.send_sems.at[len(self.sent)],
+            recv_sem=self.recv_sems.at[slot], device_id=target,
+            device_id_type=pl.DeviceIdType.MESH,
+        )
+        self.sent.append((copy, cond))
+        if cond is None:
+            copy.start()
+        else:
+            pl.when(cond)(copy.start)
+
+    def arrived(self, dst, slot, cond=None):
+        z, y, x, c = place()
+        copy = pltpu.make_async_remote_copy(
+            src_ref=dst, dst_ref=dst, send_sem=self.send_sems.at[0],
+            recv_sem=self.recv_sems.at[slot], device_id=device(z, y, x, 1 - c),
+            device_id_type=pl.DeviceIdType.MESH,
+        )
+        if cond is None:
+            copy.wait_recv()
+        else:
+            pl.when(cond)(copy.wait_recv)
+
+    def finish(self):
+        for copy, cond in self.sent:
+            if cond is None:
+                copy.wait_send()
+            else:
+                pl.when(cond)(copy.wait_send)
+
+
+def along_z(mail, block, slot, zz, k):
+    z, y, x, c = place()
+    if k == 0:
+        mail.send(block, block, slot + z, device(z + 1, y, x, c), z < NZ - 1)
+        mail.send(block, block, slot + z, device(z - 1, y, x, c), z > 0)
+    else:
+        up = zz < z
+        cond = jnp.where(up, (z < NZ - 1).astype(jnp.int32), (z > 0).astype(jnp.int32)) == 1
+        mail.send(block, block, slot + zz, device(jnp.where(up, z + 1, z - 1), y, x, c), cond)
+
+
+def gather_unit(mail, order, out, own_copy):
+    z, y, x, c = place()
+    both = pl.ds(0, 2)
+    to_x, to_y = device(z, y, 1 - x, c), device(z, 1 - y, x, c)
+    to_core = device(z, y, x, 1 - c)
+    core = []
+
+    def pair(src, slot):
+        core.append(slot)
+        mail.send(src, src, slot, to_core)
+
+    own_copy.wait()
+    if order in ("zyx", "zxy"):
+        first, second = (to_y, to_x) if order == "zyx" else (to_x, to_y)
+
+        def at(zz, one, two):
+            if order == "zyx":
+                yy = both if one is None else (1 - y if one else y)
+                return out.at[zz, yy, 1 - x if two else x, c]
+            xx = both if one is None else (1 - x if one else x)
+            return out.at[zz, 1 - y if two else y, xx, c]
+
+        s_z, s_one, s_two, s_c = mail.slot(4), mail.slot(4), mail.slot(4), mail.slot(8)
+        along_z(mail, at(z, 0, 0), s_z, z, 0)
+        mail.send(at(z, 0, 0), at(z, 0, 0), s_one + z, first)
+        for k in (1, 2, 3):
+            yield
+            zz = z_order(k, z)
+            mail.arrived(at(zz, 0, 0), s_z + zz)
+            along_z(mail, at(zz, 0, 0), s_z, zz, k)
+            mail.send(at(zz, 0, 0), at(zz, 0, 0), s_one + zz, first)
+        for k in range(4):
+            yield
+            zz = z_order(k, z)
+            mail.arrived(at(zz, 1, 0), s_one + zz)
+            mail.send(at(zz, None, 0), at(zz, None, 0), s_two + zz, second)
+            mail.send(at(zz, None, 0), at(zz, None, 0), s_c + zz, to_core)
+        for k in range(4):
+            yield
+            zz = z_order(k, z)
+            mail.arrived(at(zz, None, 1), s_two + zz)
+            mail.send(at(zz, None, 1), at(zz, None, 1), s_c + 4 + zz, to_core)
+        for k in range(8):
+            yield
+            if order == "zyx":
+                landed = out.at[z_order(k % 4, z), both, x if k < 4 else 1 - x, 1 - c]
+            else:
+                landed = out.at[z_order(k % 4, z), y if k < 4 else 1 - y, both, 1 - c]
+            mail.arrived(landed, s_c + (k // 4) * 4 + z_order(k % 4, z))
+    elif order == "xyz":
+        s_x, s_y, s_z, s_c = mail.slot(1), mail.slot(1), mail.slot(4), mail.slot(4)
+        mail.send(out.at[z, y, x, c], out.at[z, y, x, c], s_x, to_x)
+        yield
+        mail.arrived(out.at[z, y, 1 - x, c], s_x)
+        mail.send(out.at[z, y, both, c], out.at[z, y, both, c], s_y, to_y)
+        yield
+        mail.arrived(out.at[z, 1 - y, both, c], s_y)
+        for k in range(4):
+            zz = z_order(k, z)
+            block = out.at[zz, both, both, c]
+            if k:
+                yield
+                mail.arrived(block, s_z + zz)
+            along_z(mail, block, s_z, zz, k)
+            mail.send(block, block, s_c + zz, to_core)
+        for k in range(4):
+            yield
+            zz = z_order(k, z)
+            mail.arrived(out.at[zz, both, both, 1 - c], s_c + zz)
+    else:
+        s_x, s_y, s_z, s_c = mail.slot(1), mail.slot(4), mail.slot(4), mail.slot(4)
+        mail.send(out.at[z, y, x, c], out.at[z, y, x, c], s_x, to_x)
+        yield
+        mail.arrived(out.at[z, y, 1 - x, c], s_x)
+        for k in range(4):
+            zz = z_order(k, z)
+            block = out.at[zz, y, both, c]
+            if k:
+                yield
+                mail.arrived(block, s_z + zz)
+            along_z(mail, block, s_z, zz, k)
+            mail.send(block, block, s_y + zz, to_y)
+        for k in range(4):
+            yield
+            zz = z_order(k, z)
+            mail.arrived(out.at[zz, 1 - y, both, c], s_y + zz)
+            block = out.at[zz, both, both, c]
+            mail.send(block, block, s_c + zz, to_core)
+        for k in range(4):
+            yield
+            zz = z_order(k, z)
+            mail.arrived(out.at[zz, both, both, 1 - c], s_c + zz)
+
+
+def run_together(routines):
+    live = list(routines)
+    while live:
+        live = [r for r in live if next(r, "end") != "end"]
+
+
+SENDS, RECVS = 160, 160
+
+
+def gather_kernel(orders, *refs):
+    n = len(orders)
+    srcs, outs = refs[:n], refs[n : 2 * n]
+    send_sems, recv_sems, own_sems = refs[2 * n :]
+    z, y, x, c = place()
+    copies = [
+        pltpu.make_async_copy(s, o.at[z, y, x, c], own_sems.at[i])
+        for i, (s, o) in enumerate(zip(srcs, outs))
+    ]
+    for copy in copies:
+        copy.start()
+    greet()
+    mail = Mail(send_sems, recv_sems)
+    run_together([gather_unit(mail, o, out, cp) for o, out, cp in zip(orders, outs, copies)])
+    mail.finish()
+
+
+def gather_all(parts, orders, collective_id):
+    shapes = [jax.ShapeDtypeStruct((4, 2, 2, 2) + p.shape, p.dtype) for p in parts]
+    outs = pl.pallas_call(
+        functools.partial(gather_kernel, orders),
+        out_shape=shapes,
+        in_specs=[HBM] * len(parts),
+        out_specs=[HBM] * len(parts),
+        scratch_shapes=[
+            pltpu.SemaphoreType.DMA((SENDS,)),
+            pltpu.SemaphoreType.DMA((RECVS,)),
+            pltpu.SemaphoreType.DMA((len(parts),)),
+        ],
+        compiler_params=pltpu.CompilerParams(collective_id=collective_id, has_side_effects=True),
+    )(*parts)
+    return [o.reshape((32,) + p.shape) for o, p in zip(outs, parts)]
+
+
+def add_into(acc, others, cols):
+    step = 384 if cols % 384 == 0 else 128
+
+    def chunk(i, _):
+        at = pl.ds(pl.multiple_of(i * step, step), step)
+        where = tuple(slice(None) for _ in range(len(acc.shape) - 1)) + (at,)
+        total = acc[where].astype(F32)
+        for other in others:
+            total = total + other[where].astype(F32)
+        acc[where] = total.astype(acc.dtype)
+        return 0
+
+    lax.fori_loop(0, cols // step, chunk, 0)
+
+
+def reduce_unit(mail, order, grad, refs, local_sem, out):
+    acc, from_core, from_x, from_y, from_z = refs
+    cols = grad.shape[-1]
+    z, y, x, c = place()
+    both = pl.ds(0, 2)
+    to_x, to_y = device(z, y, 1 - x, c), device(z, 1 - y, x, c)
+    to_core = device(z, y, x, 1 - c)
+    own = pltpu.make_async_copy(grad.at[:, :, :, c], acc, local_sem)
+    own.start()
+    s_c, s_z = mail.slot(4), mail.slot(8)
+    for k in range(4):
+        zz = z_order(3 - k, z)
+        mail.send(grad.at[zz, :, :, 1 - c], from_core.at[zz], s_c + zz, to_core)
+
+    def line(pick, k, zz):
+        block = acc.at[(zz,) + pick]
+        if k < 3:
+            up = zz > z
+            more = jnp.where(up, (z > 0).astype(jnp.int32), (z < NZ - 1).astype(jnp.int32)) == 1
+            side = jnp.where(up, 0, 1)
+            landed = from_z.at[side, zz]
+
+            def take():
+                mail.arrived(landed, s_z + side * 4 + zz)
+                add_into(block, [landed], cols)
+
+            pl.when(more)(take)
+            mail.send(block, landed, s_z + side * 4 + zz, device(jnp.where(up, z + 1, z - 1), y, x, c))
+        else:
+            for side, there in ((0, z > 0), (1, z < NZ - 1)):
+                landed = from_z.at[side, zz]
+
+                def take(landed=landed, side=side):
+                    mail.arrived(landed, s_z + side * 4 + zz)
+                    add_into(block, [landed], cols)
+
+                pl.when(there)(take)
+
+    if order in ("zyx", "zxy"):
+        flip = order == "zxy"
+        if flip:
+            part = lambda zz, one, two: (zz, 1 - y if two else y, both if one is None else (1 - x if one else x))
+            far, near, to_far, to_near = from_y, from_x, to_y, to_x
+        else:
+            part = lambda zz, one, two: (zz, both if one is None else (1 - y if one else y), 1 - x if two else x)
+            far, near, to_far, to_near = from_x, from_y, to_x, to_y
+        s_far, s_near = mail.slot(4), mail.slot(4)
+        for k in range(4):
+            yield
+            zz = z_order(3 - k, z)
+            if k == 0:
+                own.wait()
+            mail.arrived(from_core.at[zz], s_c + zz)
+            add_into(acc.at[zz], [from_core.at[zz]], cols)
+            mail.send(acc.at[part(zz, None, 1)], far.at[zz], s_far + zz, to_far)
+        for k in range(4):
+            yield
+            zz = z_order(3 - k, z)
+            mail.arrived(far.at[zz], s_far + zz)
+            add_into(acc.at[part(zz, None, 0)], [far.at[zz]], cols)
+            mail.send(acc.at[part(zz, 1, 0)], near.at[zz], s_near + zz, to_near)
+        for k in range(4):
+            yield
+            zz = z_order(3 - k, z)
+            mail.arrived(near.at[zz], s_near + zz)
+            add_into(acc.at[part(zz, 0, 0)], [near.at[zz]], cols)
+            line((y, x), k, zz)
+    elif order == "xyz":
+        s_y, s_x = mail.slot(1), mail.slot(1)
+        for k in range(4):
+            yield
+            zz = z_order(3 - k, z)
+            if k == 0:
+                own.wait()
+            mail.arrived(from_core.at[zz], s_c + zz)
+            add_into(acc.at[zz], [from_core.at[zz]], cols)
+            line((both, both), k, zz)
+        mail.send(acc.at[z, 1 - y], from_y, s_y, to_y)
+        yield
+        mail.arrived(from_y, s_y)
+        add_into(acc.at[z, y], [from_y], cols)
+        mail.send(acc.at[z, y, 1 - x], from_x, s_x, to_x)
+        yield
+        mail.arrived(from_x, s_x)
+        add_into(acc.at[z, y, x], [from_x], cols)
+    else:
+        s_y, s_x = mail.slot(4), mail.slot(1)
+        for k in range(4):
+            yield
+            zz = z_order(3 - k, z)
+            if k == 0:
+                own.wait()
+            mail.arrived(from_core.at[zz], s_c + zz)
+            add_into(acc.at[zz], [from_core.at[zz]], cols)
+            mail.send(acc.at[zz, 1 - y], from_y.at[zz], s_y + zz, to_y)
+        for k in range(4):
+            yield
+            zz = z_order(3 - k, z)
+            mail.arrived(from_y.at[zz], s_y + zz)
+            add_into(acc.at[zz, y], [from_y.at[zz]], cols)
+            line((y, both), k, zz)
+        mail.send(acc.at[z, y, 1 - x], from_x, s_x, to_x)
+        yield
+        mail.arrived(from_x, s_x)
+        add_into(acc.at[z, y, x], [from_x], cols)
+    out[...] = acc[z, y, x].astype(F32)
+
+
+def reduce_scratch(order, shape, dtype):
+    per_x = {"zyx": (4, 2), "zxy": (4,), "xyz": (), "xzy": ()}[order]
+    per_y = {"zyx": (4,), "zxy": (4, 2), "xyz": (2,), "xzy": (4, 2)}[order]
+    per_z = {"zyx": (2, 4), "zxy": (2, 4), "xyz": (2, 4, 2, 2), "xzy": (2, 4, 2)}[order]
+    return [
+        pltpu.VMEM(lead + shape, dtype)
+        for lead in ((4, 2, 2), (4, 2, 2), per_x, per_y, per_z)
+    ]
+
+
+def reduce_kernel(orders, *refs):
+    n = len(orders)
+    grads, outs = refs[:n], refs[n : 2 * n]
+    scratch = refs[2 * n : 7 * n]
+    send_sems, recv_sems, own_sems = refs[7 * n :]
+    greet()
+    mail = Mail(send_sems, recv_sems)
+    run_together(
+        [
+            reduce_unit(mail, o, grads[i], scratch[5 * i : 5 * i + 5], own_sems.at[i], outs[i])
+            for i, o in enumerate(orders)
+        ]
+    )
+    mail.finish()
+
+
+def reduce_all(grads, orders, collective_id):
+    shapes = [jax.ShapeDtypeStruct(g.shape[1:], F32) for g in grads]
+    scratch = []
+    for g, o in zip(grads, orders):
+        scratch += reduce_scratch(o, g.shape[1:], g.dtype)
+    return pl.pallas_call(
+        functools.partial(reduce_kernel, orders),
+        out_shape=shapes,
+        in_specs=[HBM] * len(grads),
+        out_specs=[pl.BlockSpec(memory_space=pltpu.VMEM)] * len(grads),
+        scratch_shapes=scratch
+        + [
+            pltpu.SemaphoreType.DMA((SENDS,)),
+            pltpu.SemaphoreType.DMA((RECVS,)),
+            pltpu.SemaphoreType.DMA((len(grads),)),
+        ],
+        compiler_params=pltpu.CompilerParams(
+            collective_id=collective_id, has_side_effects=True, vmem_limit_bytes=60 << 20
+        ),
+    )(*[g.reshape((4, 2, 2, 2) + g.shape[1:]) for g in grads])
+
+
+def swap(values, distance):
+    return lax.ppermute(values, "seq", [(s, s ^ distance) for s in range(4)])
+
+
+def to_one_sequence(values):
+    _, _, x, _ = place()
+    mine = lax.dynamic_index_in_dim(values, x, 0, keepdims=False)
+    theirs = swap(lax.dynamic_index_in_dim(values, 1 - x, 0, keepdims=False), 2)
+    low = x == 0
+    return jnp.stack([jnp.where(low, mine, theirs), jnp.where(low, theirs, mine)])
+
+
+VECTORS = (72, 24, 24, 24, 96, 24, 24, 24)
+
+
+def pack_vectors(parts):
+    joined = jnp.concatenate(parts, axis=-1)
+    lead = joined.shape[:-1]
+    joined = jnp.pad(joined, [(0, 0)] * len(lead) + [(0, 2048 - joined.shape[-1])])
+    return joined.reshape(lead + (16, 128))
+
+
+def unpack_vectors(packed):
+    joined = packed.reshape(packed.shape[:-2] + (2048,))
+    out, at = [], 0
+    for n in VECTORS:
+        out.append(joined[..., at : at + n])
+        at += n
+    return out
+
+
+ORDERS = ("xyz", "xzy", "zyx", "zyx", "xyz", "zyx", "zxy")
+
+
+def fast_device(*args):
+    (tokens, segment_ids, w_qkv, b_qkv, w_out, b_out, gain_one, shift_one) = args[:8]
+    (w_in, b_in, w_back, b_back, gain_two, shift_two, out_grad) = args[8:]
+    z, y, x, c = place()
+    rows = tokens.shape[1]
+    count = 2 * rows
+    vectors = pack_vectors([b_qkv, b_out, gain_one, shift_one, b_in, b_back, gain_two, shift_two])
+    w_q, w_k, w_v, vectors, w_out, w_in, w_back = gather_all(
+        [w_qkv[:, :D], w_qkv[:, D : 2 * D], w_qkv[:, 2 * D :], vectors, w_out, w_in, w_back],
+        ORDERS, 0,
+    )
+    w_q, w_k, w_v, w_out, w_in, w_back = [
+        w.reshape(-1, w.shape[-1]) for w in (w_q, w_k, w_v, w_out, w_in, w_back)
+    ]
+    b_qkv, b_out, gain_one, shift_one, b_in, b_back, gain_two, shift_two = [
+        v.reshape(-1).astype(F32) for v in unpack_vectors(vectors)
+    ]
+    ids = lax.dynamic_index_in_dim(segment_ids, x, 0)
+    length = ids.shape[1]
+    cos_all, sin_all = rotary_tables(ids, 0, length)
+
+    def own_rows(values):
+        halves = values.reshape((2, 2, rows) + values.shape[2:])
+        return lax.dynamic_index_in_dim(halves, c, 1, keepdims=False).reshape(
+            (1, count) + values.shape[2:]
+        )
+
+    def both_cores(own):
+        other = swap(own, 1)
+        low = c == 0
+        one = jnp.where(low, own, other).reshape(2, 1, rows, own.shape[-1])
+        two = jnp.where(low, other, own).reshape(2, 1, rows, own.shape[-1])
+        return jnp.concatenate([one, two], axis=1).reshape(1, 2 * count, own.shape[-1])
+
+    own_ids, cos_part, sin_part = own_rows(ids), own_rows(cos_all), own_rows(sin_all)
+    same_doc = own_ids[:, :, None] == ids[:, None, :]
+
+    tok = to_one_sequence(tokens).reshape(count, D)
+    grad_rows = to_one_sequence(out_grad).reshape(count, D)
+    query = rotate((mm(tok, w_q) + b_qkv[:D])[None], cos_part, sin_part).astype(BF)
+    key = rotate((mm(tok, w_k) + b_qkv[D : 2 * D])[None], cos_part, sin_part).astype(BF)
+    value = (mm(tok, w_v) + b_qkv[2 * D :]).astype(BF)[None]
+    key_all, value_all = both_cores(key), both_cores(value)
+    scores = scores_of(query, key_all, same_doc)
+    highest = jnp.max(scores, axis=-1, keepdims=True)
+    exponent = jnp.exp(scores - highest)
+    total = jnp.sum(exponent, axis=-1, keepdims=True)
+    log_total = highest + jnp.log(total)
+    mixed = jnp.einsum(
+        "bhqk,bkhd->bqhd", (exponent / total).astype(BF), heads(value_all),
+        preferred_element_type=F32,
+    ).astype(BF).reshape(count, D)
+    first_sum = tok.astype(F32) + mm(mixed, w_out) + b_out
+    normed = layer_norm(first_sum, gain_one, shift_one)
+    normed_low = normed.astype(BF)
+    inner = mm(normed_low, w_in) + b_in
+    active = gelu_exact(inner).astype(BF)
+    second_sum = normed + mm(active, w_back) + b_back
+    result, pull_two = jax.vjp(layer_norm, second_sum, gain_two, shift_two)
+    layer_out = to_one_sequence(result.astype(BF).reshape(2, rows, D))
+
+    d_second_sum, d_gain_two, d_shift_two = pull_two(grad_rows.astype(F32))
+    d_second = d_second_sum.astype(BF)
+    d_b_back = jnp.sum(d_second.astype(F32), axis=0)
+    d_w_back = jnp.einsum("qf,qd->fd", active, d_second, preferred_element_type=F32).astype(BF)
+    d_active = jnp.einsum("qd,fd->qf", d_second, w_back, preferred_element_type=F32)
+    d_inner = jax.vjp(gelu_exact, inner)[1](d_active)[0].astype(BF)
+    d_b_in = jnp.sum(d_inner.astype(F32), axis=0)
+    d_w_in = jnp.einsum("qd,qf->df", normed_low, d_inner, preferred_element_type=F32).astype(BF)
+    d_normed = d_second_sum + jnp.einsum("qf,df->qd", d_inner, w_in, preferred_element_type=F32)
+    d_first_sum, d_gain_one, d_shift_one = jax.vjp(layer_norm, first_sum, gain_one, shift_one)[1](
+        d_normed
+    )
+    d_branch = d_first_sum.astype(BF)
+    d_b_out = jnp.sum(d_branch.astype(F32), axis=0)
+    d_w_out = jnp.einsum("qd,qe->de", mixed, d_branch, preferred_element_type=F32).astype(BF)
+    d_mixed = jnp.einsum("qe,de->qd", d_branch, w_out, preferred_element_type=F32).astype(BF)[None]
+
+    attention = jnp.exp(scores_of(query, key_all, same_doc) - log_total)
+    d_attention = jnp.einsum(
+        "bqhd,bkhd->bhqk", heads(d_mixed), heads(value_all), preferred_element_type=F32
+    )
+    inner_sum = jnp.sum(d_attention * attention, axis=-1, keepdims=True)
+    d_scores = (attention * (d_attention - inner_sum) * HD ** (-0.5)).astype(BF)
+    d_query = jnp.einsum(
+        "bhqk,bkhd->bqhd", d_scores, heads(key_all), preferred_element_type=F32
+    ).reshape(1, count, D)
+
+    def sum_cores(partial):
+        quarters = partial.reshape(2, 2, rows, D)
+        mine = lax.dynamic_index_in_dim(quarters, c, 1, keepdims=False)
+        theirs = lax.dynamic_index_in_dim(quarters, 1 - c, 1, keepdims=False).astype(BF)
+        return (mine + swap(theirs, 1).astype(F32)).reshape(1, count, D)
+
+    d_value = sum_cores(jnp.einsum(
+        "bhqk,bqhd->bkhd", attention.astype(BF), heads(d_mixed), preferred_element_type=F32
+    ).reshape(1, 2 * count, D)).astype(BF)[0]
+    d_key = sum_cores(jnp.einsum(
+        "bhqk,bqhd->bkhd", d_scores, heads(query), preferred_element_type=F32
+    ).reshape(1, 2 * count, D))
+    d_query = rotate(d_query, cos_part, -sin_part).astype(BF)[0]
+    d_key = rotate(d_key, cos_part, -sin_part).astype(BF)[0]
+    d_b_qkv = jnp.concatenate([jnp.sum(d.astype(F32), axis=0) for d in (d_query, d_key, d_value)])
+    d_w_q, d_w_k, d_w_v = [
+        jnp.einsum("qd,qe->de", tok, d, preferred_element_type=F32).astype(BF)
+        for d in (d_query, d_key, d_value)
+    ]
+    d_tokens = d_first_sum
+    for d, w in ((d_query, w_q), (d_key, w_k), (d_value, w_v)):
+        d_tokens = d_tokens + jnp.einsum("qe,de->qd", d, w, preferred_element_type=F32)
+    d_tokens = to_one_sequence(d_tokens.astype(BF).reshape(2, rows, D)).astype(F32)
+    small = pack_vectors([
+        v.reshape(32, -1)
+        for v in (d_b_qkv, d_b_out, d_gain_one, d_shift_one, d_b_in, d_b_back, d_gain_two, d_shift_two)
+    ]).astype(BF)
+    d_w_q, d_w_k, d_w_v, d_w_out, d_w_in, d_w_back = [
+        g.reshape(32, -1, g.shape[-1]) for g in (d_w_q, d_w_k, d_w_v, d_w_out, d_w_in, d_w_back)
+    ]
+    d_w_q, d_w_k, d_w_v, small, d_w_out, d_w_in, d_w_back = reduce_all(
+        [d_w_q, d_w_k, d_w_v, small, d_w_out, d_w_in, d_w_back], ORDERS, 1
+    )
+    small = unpack_vectors(small)
+    return (
+        layer_out, d_tokens, jnp.concatenate([d_w_q, d_w_k, d_w_v], axis=1), small[0], d_w_out,
+        small[1], small[2], small[3], d_w_in, small[4], d_w_back, small[5], small[6], small[7],
+    )
+
+
 def solution(mesh):
     devices = mesh.shape["dp"] * mesh.shape["seq"]
+    fast = mesh.shape["dp"] == 8 and mesh.shape["seq"] == 4
     rows3 = P("dp", "seq", None)
     mat, vec = P(ALL, None), P(ALL)
     params = (mat, vec, mat, vec, vec, vec, mat, vec, mat, vec, vec, vec)
     return jax.shard_map(
-        lambda *args: on_device(devices, *args),
+        fast_device if fast else (lambda *args: on_device(devices, *args)),
         mesh=mesh,
         in_specs=(rows3, P("dp", None)) + params + (rows3,),
         out_specs=(rows3, rows3) + params,

time: 961 us -> 582 us (0.61)
  waiting for transfers between devices: 535 us -> 3.96 us
  Pallas kernels: 0 us -> 171 us
  blocking collectives: 82.8 us -> 0 us
  local copies, waits for them, and re-layouts: 53 us -> 115 us
  other arithmetic: 34.1 us -> 53.7 us
  between operations: 15.2 us -> 2.13 us
  matrix products: 233 us -> 221 us
    reduce_scatter x5 -> x0, waiting for transfers between devices: 292 us -> none  [the longest x3 292 us: scatter(): lax.psum_scatter(grad.astype(BF), ALL, scatter_dimension=0, tiled=True)]
    all_gather x6 -> x0, waiting for transfers between devices: 183 us -> none  [the longest x4 159 us: gather(): return lax.all_gather(local, ALL, axis=0, tiled=True)]
    pallas_call x0 -> x2, Pallas kernels: none -> 171 us  [the longest x1 89.4 us: gather_all(): pl.pallas_call(functools.partial(gather_kernel, orders), out_shape=shapes...]
    unnamed x2 -> x0, blocking collectives: 82.8 us -> none
    unnamed x13 -> x0, waiting for transfers between devices: 59.7 us -> none
    dynamic_slice x1 -> x20, local copies, waits for them, and re-layouts: 0.01 us -> 28.7 us  [the longest x4 16.9 us: sum_cores(): mine = lax.dynamic_index_in_dim(quarters, c, 1, keepdims=False)]
    another operation x1 -> x9, local copies, waits for them, and re-layouts: 2.91 us -> 19.6 us  [the longest x2 11.3 us: sum_cores(): quarters = partial.reshape(2, 2, rows, D)]
    dot_general x13 -> x17, matrix products: 186 us -> 173 us  [the longest x1 52.1 us: fast_device(): jnp.einsum('bhqk,bkhd->bqhd', d_scores, heads(key_all), preferred_element...]
  transfers between devices with their start and end apart: 12 -> 8, of which waited for: 10 -> 1; matrix products, arithmetic and copies ran while one was open for 21% -> 21% of each run, Pallas kernels for 0% -> 30%
where the time goes in v2:
time: 582 us; the launch traced here: 573 us
  matrix products  221 us (38%)
  Pallas kernels  171 us (29%)
  local copies, waits for them, and re-layouts  115 us (20%)
  other arithmetic  53.7 us (9%)
    pallas_call x1, Pallas kernels, gather_all(): pl.pallas_call(functools.partial(gather_kernel, orders), out_shape=shapes...  89.4 us
    pallas_call x1, Pallas kernels, reduce_all(): pl.pallas_call(functools.partial(reduce_kernel, orders), out_shape=shapes...  81.7 us
    dot_general x1, matrix products, fast_device(): jnp.einsum('bhqk,bkhd->bqhd', d_scores, heads(key_all), preferred_element...  52.1 us
    dot_general x1, matrix products, fast_device(): jnp.einsum('bhqk,bqhd->bkhd', d_scores, heads(query), preferred_element_t...  46.9 us
    dot_general x6, matrix products, mm(): return jnp.dot(a, b, preferred_element_type=F32)  34.1 us
    unnamed x118, local copies, waits for them, and re-layouts  19.6 us
    dynamic_slice x4, local copies, waits for them, and re-layouts, sum_cores(): mine = lax.dynamic_index_in_dim(quarters, c, 1, keepdims=False)  16.9 us
    dot_general x1, matrix products, scores_of(): jnp.einsum('bqhd,bkhd->bhqk', heads(query), heads(key_all), preferred_ele...  14.4 us
  transfers between devices with their start and end apart: 8, of which 1 were waited for; matrix products, arithmetic and copies ran while one was open for 21% of the time, Pallas kernels for 30%

profile of v2, /device:TPU:0, one launch (start us, length us, event | category | flops | bytes accessed | tf_op | source)
XLA Modules:
  0.0 572.6 jit_solution(12358562397095287602)
XLA Ops:
  9.4 89.4 %shard_map.254 = (bf16[4,2,2,2,24,768]{5,4,3,2,1,0:T(8,128)(2,1)}, bf16[4,2,2,2,24,768]{5,4,3,2,1,0:T(8,128)(2,1)}, bf16[4,2,2,2,24,768]{5,4,3,2,1,0:T(8,128)(2,...) custom-call(bf16[24,768]{1,0:T(8,128)(2,1)} %get-tuple-element.139.r, ...), custom_call_target="tpu_custom_call" | custom-call | tf_op jit(solution)/shard_map/pallas_call | solution.py:406
  111.4 3.4 convolution_add_fusion.1
  118.8 5.8 %subtract_convert_fusion.2 = (bf16[1,512,12,32,1]{1,4,3,2,0:T(2,128)(2,1)S(1)}, bf16[1,512,12,32,1]{1,4,3,2,0:T(2,128)(2,1)S(1)}, bf16[1,512,12,32,1]{1,4,3,2,0:T(2,128)(2,1)S(1)}, bf16[1,512,12,32,1]{1,4,3,2,0:T(2,128)(2,1)S(1)}) fusion(f32[1,512,12,32,2]{1,4,3,2,0:T(2,128)S(1)} %reshape_broadcast_in_dim.9, f32[512,32]{0,1:T(8,128)} %bitcast.246, ...), kind=kLoop, calls=%fused_computation.87 | loop fusion | flops 3145728 | bytes 4849664 | tf_op jit(solution)/shard_map/convert.36
  137.3 3.2 fusion.33
  150.8 3.8 reshape.707
  159.3 3.2 reshape.699
  162.5 14.4 %fusion.3 = (f32[12,512]{1,0:T(8,128)S(1)}, f32[12,512,1024]{2,1,0:T(8,128)}) fusion(pred[512,1024]{1,0:T(8,128)(4,1)} %broadcast_compare_fusion, bf16[512,12,64]{0,2,1:T(8,128)(2,1)} %convert_element_type.317, bf16[1024,12,64]{0,2,1:T(8,128)(2,1)} %reshape.707), kind=kOutput, calls=%fused_computation.9 | convolution fusion | flops 824174592 | bytes 28073984 | tf_op jit(solution)/shard_map/bqhd,bkhd->bhqk/dot_general | solution.py:90
  177.0 12.3 %fusion.2 = f32[12,512]{1,0:T(8,128)S(1)} fusion(f32[12,512,1024]{2,1,0:T(8,128)} %get-tuple-element.151, f32[12,512]{1,0:T(8,128)S(1)} %get-tuple-element.150, pred[512,1024]{1,0:T(8,128)(4,1)S(1)} %copy-done.8), kind=kLoop, calls=%fused_computation.8 | loop fusion | flops 25159680 | bytes 25739264 | tf_op jit(solution)/shard_map/reduce_sum | solution.py:672
  189.3 3.0 copy-done
  192.3 8.5 %fusion.32 = bf16[12,64,512]{2,1,0:T(8,128)(2,1)} fusion(bf16[1024,12,64]{0,2,1:T(8,128)(2,1)S(1)} %reshape.699, f32[12,512,1024]{2,1,0:T(8,128)S(1)} %copy-done, f32[12,512]{1,0:T(8,128)S(1)} %fusion.2, f32[12,512]{1,0:T(8,128)S(1)} %get-tuple-element.150, pred[512,1024]{1,0:T(8,128)(4,1)S(1)} %copy-done.8), kind=kOutput, calls=%fused_computation.68 | convolution fusion | flops 837156864 | bytes 28098560 | tf_op jit(solution)/shard_map/bhqk,bkhd->bqhd/dot_general | solution.py:674
  203.9 19.8 %multiply_convert_fusion.1 = (bf16[512,3072]{1,0:T(8,128)(2,1)S(1)}, f32[512,3072]{1,0:T(8,128)}, f32[512,3072]{1,0:T(8,128)}) fusion(f32[3072]{0:T(1024)S(1)} %copy-done.33, bf16[768,3072]{1,0:T(8,128)(2,1)} %bitcast.264, f32[512,768]{1,0:T(8,128)S(1)} %get-tuple-element.153, f32[768]{0:T(1024)S(1)} %copy-done.34, f32[768]{0:T(1024)S(1)} %copy-done.32, ...), kind=kOutput, calls=%fused_computation.18 | convolution fusion | flops 2521694208 | bytes 22042624 | tf_op jit(solution)/shard_map/dot_general | solution.py:20
  229.3 9.4 %fusion.65 = (bf16[3072]{0:T(1024)(128)(2,1)S(1)}, bf16[512,3072]{1,0:T(8,128)(2,1)}) fusion(f32[512,3072]{1,0:T(8,128)} %get-tuple-element.94, f32[512,3072]{1,0:T(8,128)} %get-tuple-element.154, f32[3072]{0:T(1024)S(1)} %copy-done.33, bf16[512,768]{1,0:T(8,128)(2,1)S(1)} %get-tuple-element.78, bf16[3072,768]{1,0:T(8,128)(2,1)S(1)} %bitcast.271), kind=kOutput, calls=%fused_computation.172 | convolution fusion | flops 2441081856 | bytes 21252096 | tf_op jit(solution)/shard_map/qd,fd->qf/dot_general | solution.py:691
  238.8 5.1 multiply_reduce_fusion.1
  249.6 11.4 %fusion.80 = f32[12,512,1024]{2,1,0:T(8,128)} fusion(bf16[512,12,64]{0,2,1:T(8,128)(2,1)} %bitcast.219, bf16[1024,12,64]{0,2,1:T(8,128)(2,1)S(1)} %reshape.699), kind=kOutput, calls=%fused_computation.185 | convolution fusion | flops 805306368 | bytes 27525120 | tf_op jit(solution)/shard_map/bqhd,bkhd->bhqk/dot_general | solution.py:705
  261.0 52.1 %fusion.29 = f32[1,512,12,64]{1,3,2,0:T(8,128)} fusion(bf16[1024,12,64]{0,2,1:T(8,128)(2,1)} %reshape.707, f32[12,512,1024]{2,1,0:T(8,128)} %fusion.80, f32[12,512]{1,0:T(8,128)S(1)} %log_add_fusion, f32[12,512,1024]{2,1,0:T(8,128)} %get-tuple-element.151, pred[512,1024]{1,0:T(8,128)(4,1)} %broadcast_compare_fusion), kind=kOutput, calls=%fused_computation.61 | convolution fusion | flops 874519552 | bytes 54026240 | tf_op jit(solution)/shard_map/bhqk,bkhd->bqhd/dot_general | solution.py:710
  313.1 46.9 %fusion.21 = f32[1,1024,12,64]{1,3,2,0:T(8,128)} fusion(bf16[512,12,64]{0,2,1:T(8,128)(2,1)} %convert_element_type.317, f32[12,512,1024]{2,1,0:T(8,128)} %fusion.80, f32[12,512]{1,0:T(8,128)S(1)} %log_add_fusion, f32[12,512,1024]{2,1,0:T(8,128)} %get-tuple-element.151, pred[512,1024]{1,0:T(8,128)(4,1)S(1)} %copy-done.9), kind=kOutput, calls=%fused_computation.37 | convolution fusion | flops 874519552 | bytes 54812672 | tf_op jit(solution)/shard_map/bhqk,bqhd->bkhd/dot_general | solution.py:723
  359.9 13.2 %fusion.24 = f32[1,1024,12,64]{1,3,2,0:T(8,128)} fusion(bf16[512,12,64]{0,2,1:T(8,128)(2,1)S(1)} %bitcast.220, f32[12,512]{1,0:T(8,128)S(1)} %log_add_fusion, f32[12,512,1024]{2,1,0:T(8,128)} %get-tuple-element.151, pred[512,1024]{1,0:T(8,128)(4,1)S(1)} %copy-done.9), kind=kOutput, calls=%fused_computation.38 | convolution fusion | flops 830472192 | bytes 29646848 | tf_op jit(solution)/shard_map/bhqk,bqhd->bkhd/dot_general | solution.py:720
  373.1 5.6 reshape_reshape.64
  378.7 4.6 constant_dynamic-slice_fusion.5
  385.8 5.7 %reshape_reshape.66 = f32[2,2,256,768]{2,1,0,3:T(2,128)} reshape(f32[1,1024,12,64]{1,3,2,0:T(8,128)} %fusion.24) | data formatting | bytes 6291456 | tf_op jit(solution)/shard_map/reshape;reshape | solution.py:715
  391.6 3.5 constant_dynamic-slice_fusion.2
  397.5 6.7 %convolution_convert_fusion = bf16[3072,768]{1,0:T(8,128)(2,1)} fusion(bf16[512,3072]{1,0:T(8,128)(2,1)} %copy-done.48, bf16[512,768]{1,0:T(8,128)(2,1)S(1)} %copy-done.22), kind=kOutput, calls=%fused_computation.32 | convolution fusion | flops 2418278400 | bytes 8650752 | tf_op jit(solution)/shard_map/qf,qd->fd/dot_general | solution.py:690
  407.2 4.8 copy.69
  412.1 4.7 copy.78
  420.1 5.0 copy.72
  425.7 3.3 convolution_convert_fusion.2
  429.0 4.9 convolution_convert_fusion.1
  442.2 6.5 %subtract_convert_fusion.1 = (bf16[1,512,12,32,1]{1,4,3,2,0:T(2,128)(2,1)S(1)}, bf16[1,512,12,32,1]{1,4,3,2,0:T(2,128)(2,1)S(1)}, bf16[1,512,12,32,1]{1,4,3,2,0:T(2,128)(2,1)S(1)}, bf16[1,512,12,32,1]{1,4,3,2,0:T(2,128)(2,1)S(1)}) fusion(f32[1,512,12,32,2]{1,4,3,2,0:T(2,128)} %reshape_reshape.63, f32[512,32]{0,1:T(8,128)S(1)} %copy-done.27, ...), kind=kLoop, calls=%fused_computation.85 | loop fusion | flops 3145728 | bytes 4849664 | tf_op jit(solution)/shard_map/convert.34
  457.5 3.3 convert_element_type.347
  460.9 3.3 convolution_convert_fusion.4
  474.5 81.7 %shard_map.255 = (f32[24,768]{1,0:T(8,128)}, f32[24,768]{1,0:T(8,128)}, f32[24,768]{1,0:T(8,128)}, f32[16,128]{1,0:T(8,128)}, f32[24,768]{1,0:T(8,128)}, /*index=5*/f32[24,3072]{1,0:T(8,128)}, f32[96,768]{1,0:T(8,128)}) custom-call(bf16[4,2,2,2,24,768]{5,4,3,2,1,0:T(8,128)(2,1)} %bitcast.231, bf16[4,2,2,2,24,768]{5,4,3,2,1,0:T(8,128)(2,1)} %bitcast.232, ...), custom_call_target="tpu_custom_call" | custom-call | tf_op jit(solution)/shard_map/pallas_call | solution.py:575
  564.4 3.9 collective-permute-done.7
  (258 shorter events, 118.2 us)
Async XLA Ops:
  0.6 6.7 %copy-start.31 = (s32[2,1024]{1,0:T(2,128)S(1)}, s32[2,1024]{1,0:T(2,128)}, u32[]{:S(2)}) copy-start(s32[2,1024]{1,0:T(2,128)} %param.16) | copy-start | bytes 24580
  0.7 7.4 %copy-start.28 = (bf16[24,2304]{1,0:T(8,128)(2,1)S(1)}, bf16[24,2304]{1,0:T(8,128)(2,1)}, u32[]{:S(2)}) copy-start(bf16[24,2304]{1,0:T(8,128)(2,1)} %param.17) | copy-start | bytes 331780
  0.7 8.0 %copy-start.36 = (bf16[72]{0:T(256)(128)(2,1)S(1)}, bf16[72]{0:T(256)(128)(2,1)}, u32[]{:S(2)}) copy-start(bf16[72]{0:T(256)(128)(2,1)} %param.18) | copy-start | bytes 436
  0.7 8.0 %copy-start.37 = (bf16[24]{0:T(256)(128)(2,1)S(1)}, bf16[24]{0:T(256)(128)(2,1)}, u32[]{:S(2)}) copy-start(bf16[24]{0:T(256)(128)(2,1)} %param.20) | copy-start | bytes 148
  0.7 8.0 %copy-start.38 = (bf16[24]{0:T(256)(128)(2,1)S(1)}, bf16[24]{0:T(256)(128)(2,1)}, u32[]{:S(2)}) copy-start(bf16[24]{0:T(256)(128)(2,1)} %param.21) | copy-start | bytes 148
  0.7 8.0 %copy-start.39 = (bf16[24]{0:T(256)(128)(2,1)S(1)}, bf16[24]{0:T(256)(128)(2,1)}, u32[]{:S(2)}) copy-start(bf16[24]{0:T(256)(128)(2,1)} %param.22) | copy-start | bytes 148
  0.7 8.0 %copy-start.40 = (bf16[96]{0:T(256)(128)(2,1)S(1)}, bf16[96]{0:T(256)(128)(2,1)}, u32[]{:S(2)}) copy-start(bf16[96]{0:T(256)(128)(2,1)} %param.24) | copy-start | bytes 580
  0.7 8.0 %copy-start.41 = (bf16[24]{0:T(256)(128)(2,1)S(1)}, bf16[24]{0:T(256)(128)(2,1)}, u32[]{:S(2)}) copy-start(bf16[24]{0:T(256)(128)(2,1)} %param.26) | copy-start | bytes 148
  0.7 8.0 %copy-start.42 = (bf16[24]{0:T(256)(128)(2,1)S(1)}, bf16[24]{0:T(256)(128)(2,1)}, u32[]{:S(2)}) copy-start(bf16[24]{0:T(256)(128)(2,1)} %param.27) | copy-start | bytes 148
  0.7 8.0 %copy-start.43 = (bf16[24]{0:T(256)(128)(2,1)S(1)}, bf16[24]{0:T(256)(128)(2,1)}, u32[]{:S(2)}) copy-start(bf16[24]{0:T(256)(128)(2,1)} %param.28) | copy-start | bytes 148
  2.2 104.2 %collective-permute-start = (bf16[256,768]{0,1:T(8,128)(2,1)S(1)}, bf16[256,768]{0,1:T(8,128)(2,1)S(1)}, u32[]{:S(2)}, u32[]{:S(2)}) collective-permute-start(bf16[256,768]{0,1:T(8,128)(2,1)S(1)} %bitcast.249), channel_id=1, source_target_pairs={{0,2},{1,3},{2,0},{3,1},{4,6},{5,7},{6,4},{7,5},{8,10},{9,11},{10,... | collective-permute-start | bytes 1179656 | tf_op jit(solution)/shard_map/ppermute | solution.py:593
  7.3 136.2 %collective-permute-start.4 = (bf16[256,768]{0,1:T(8,128)(2,1)}, bf16[256,768]{0,1:T(8,128)(2,1)}, u32[]{:S(2)}, u32[]{:S(2)}) collective-permute-start(bf16[256,768]{0,1:T(8,128)(2,1)} %bitcast.29), channel_id=1, source_target_pairs={{0,2},{1,3},{2,0},{3,1},{4,6},{5,7},{6,4},{7,5},{8,10},{9,11},{10,... | collective-permute-start | bytes 1179656 | tf_op jit(solution)/shard_map/ppermute | solution.py:593
  127.8 18.4 %collective-permute-start.2 = (bf16[1,512,768]{2,1,0:T(8,128)(2,1)}, bf16[1,512,768]{2,1,0:T(8,128)(2,1)}, u32[]{:S(2)}, u32[]{:S(2)}) collective-permute-start(bf16[1,512,768]{2,1,0:T(8,128)(2,1)} %copy.60), channel_id=1, source_target_pairs={{0,1},{1,0},{2,3},{3,2},{4,5},{5,4},{6,7},{7,6},{8,9},{9,8},{10,11... | collective-permute-start | bytes 2359304 | tf_op jit(solution)/shard_map/ppermute | solution.py:593
  140.5 14.2 %collective-permute-start.1 = (bf16[1,512,768]{2,1,0:T(8,128)(2,1)}, bf16[1,512,768]{2,1,0:T(8,128)(2,1)}, u32[]{:S(2)}, u32[]{:S(2)}) collective-permute-start(bf16[1,512,768]{2,1,0:T(8,128)(2,1)} %fusion.33), channel_id=1, source_target_pairs={{0,1},{1,0},{2,3},{3,2},{4,5},{5,4},{6,7},{7,6},{8,9},{9,8},{10,11... | collective-permute-start | bytes 2359304 | tf_op jit(solution)/shard_map/ppermute | solution.py:593
  162.5 14.4 %copy-start.8 = (pred[512,1024]{1,0:T(8,128)(4,1)S(1)}, pred[512,1024]{1,0:T(8,128)(4,1)}, u32[]{:S(2)}) copy-start(pred[512,1024]{1,0:T(8,128)(4,1)} %broadcast_compare_fusion) | copy-start | bytes 1572868
  176.9 15.4 %copy-start = (f32[12,512,1024]{2,1,0:T(8,128)S(1)}, f32[12,512,1024]{2,1,0:T(8,128)}, u32[]{:S(2)}) copy-start(f32[12,512,1024]{2,1,0:T(8,128)} %get-tuple-element.151) | copy-start | bytes 75497472
  192.3 8.5 %copy-start.16 = (bf16[2,256,768]{2,1,0:T(8,128)(2,1)S(1)}, bf16[2,256,768]{2,1,0:T(8,128)(2,1)}, u32[]{:S(2)}) copy-start(bf16[2,256,768]{2,1,0:T(8,128)(2,1)} %copy.54) | copy-start | bytes 2359300
  192.3 8.5 %copy-start.35 = (f32[768]{0:T(1024)S(1)}, f32[768]{0:T(1024)}, u32[]{:S(2)}) copy-start(f32[768]{0:T(1024)} %reshape.722) | copy-start | bytes 9220
  200.9 22.8 %slice-start.2 = ((s8[4718592]{0:T(1024)(128)(4,1)}), s8[4194304]{0:T(1024)(128)(4,1)S(1)}, s32[]{:S(2)}) async-start(s8[4718592]{0:T(1024)(128)(4,1)} %bitcast.268), calls=%async_computation.2 | async-start | bytes 8388608
  203.5 40.4 %copy-start.4 = (f32[512,768]{1,0:T(8,128)}, f32[512,768]{1,0:T(8,128)S(1)}, u32[]{:S(2)}) copy-start(f32[512,768]{1,0:T(8,128)S(1)} %get-tuple-element.153) | copy-start | bytes 4718596
  203.8 19.8 %slice-start.3 = ((s8[4718592]{0:T(1024)(128)(4,1)}), s8[524288]{0:T(1024)(128)(4,1)S(1)}, s32[]{:S(2)}) async-start(s8[4718592]{0:T(1024)(128)(4,1)} %bitcast.268), calls=%async_computation.3 | async-start | bytes 1048576
  227.5 11.3 %slice-start = ((s8[4718592]{0:T(1024)(128)(4,1)}), s8[4194304]{0:T(1024)(128)(4,1)S(1)}, s32[]{:S(2)}) async-start(s8[4718592]{0:T(1024)(128)(4,1)} %bitcast.265), calls=%async_computation | async-start | bytes 8388608
  229.3 9.5 %copy-start.21 = (bf16[512,768]{1,0:T(8,128)(2,1)}, bf16[512,768]{1,0:T(8,128)(2,1)S(1)}, u32[]{:S(2)}) copy-start(bf16[512,768]{1,0:T(8,128)(2,1)S(1)} %get-tuple-element.78) | copy-start | bytes 2359300
  229.3 9.5 %slice-start.1 = ((s8[4718592]{0:T(1024)(128)(4,1)}), s8[524288]{0:T(1024)(128)(4,1)S(1)}, s32[]{:S(2)}) async-start(s8[4718592]{0:T(1024)(128)(4,1)} %bitcast.265), calls=%async_computation.1 | async-start | bytes 1048576
  261.0 52.1 %copy-start.9 = (pred[512,1024]{1,0:T(8,128)(4,1)S(1)}, pred[512,1024]{1,0:T(8,128)(4,1)}, u32[]{:S(2)}) copy-start(pred[512,1024]{1,0:T(8,128)(4,1)} %broadcast_compare_fusion) | copy-start | bytes 1572868
  313.1 46.9 %copy-start.3 = (bf16[512,768]{0,1:T(8,128)(2,1)S(1)}, bf16[512,768]{0,1:T(8,128)(2,1)}, u32[]{:S(2)}) copy-start(bf16[512,768]{0,1:T(8,128)(2,1)} %copy.68) | copy-start | bytes 2359300
  416.7 17.2 %collective-permute-start.5 = (bf16[2,256,768]{2,1,0:T(8,128)(2,1)}, bf16[2,256,768]{2,1,0:T(8,128)(2,1)}, u32[]{:S(2)}, u32[]{:S(2)}) collective-permute-start(bf16[2,256,768]{2,1,0:T(8,128)(2,1)} %bitcast.243), channel_id=1, source_target_pairs={{0,1},{1,0},{2,3},{3,2},{4,5},{5,4},{6,7},{7,6},{8,9},{9,8},{10,11... | collective-permute-start | bytes 2359304 | tf_op jit(solution)/shard_map/ppermute | solution.py:593
  420.1 8.9 %copy-start.5 = (f32[512,768]{1,0:T(8,128)S(1)}, f32[512,768]{1,0:T(8,128)}, u32[]{:S(2)}) copy-start(f32[512,768]{1,0:T(8,128)} %copy-done.4) | copy-start | bytes 4718596
  420.1 47.7 %collective-permute-start.6 = (bf16[2,256,768]{2,1,0:T(8,128)(2,1)}, bf16[2,256,768]{2,1,0:T(8,128)(2,1)}, u32[]{:S(2)}, u32[]{:S(2)}) collective-permute-start(bf16[2,256,768]{2,1,0:T(8,128)(2,1)} %bitcast.242), channel_id=1, source_target_pairs={{0,1},{1,0},{2,3},{3,2},{4,5},{5,4},{6,7},{7,6},{8,9},{9,8},{10,11... | collective-permute-start | bytes 2359304 | tf_op jit(solution)/shard_map/ppermute | solution.py:593
  457.5 6.7 %copy-start.17 = (bf16[2,256,768]{2,1,0:T(8,128)(2,1)S(1)}, bf16[2,256,768]{2,1,0:T(8,128)(2,1)}, u32[]{:S(2)}) copy-start(bf16[2,256,768]{2,1,0:T(8,128)(2,1)} %copy.54) | copy-start | bytes 2359300
  472.6 90.5 %collective-permute-start.3 = (bf16[256,768]{0,1:T(8,128)(2,1)S(1)}, bf16[256,768]{0,1:T(8,128)(2,1)S(1)}, u32[]{:S(2)}, u32[]{:S(2)}) collective-permute-start(bf16[256,768]{0,1:T(8,128)(2,1)S(1)} %bitcast.250), channel_id=1, source_target_pairs={{0,2},{1,3},{2,0},{3,1},{4,6},{5,7},{6,4},{7,5},{8,10},{9,11},{10,... | collective-permute-start | bytes 1179656 | tf_op jit(solution)/shard_map/ppermute | solution.py:593
  560.5 7.8 %collective-permute-start.7 = (bf16[256,768]{0,1:T(8,128)(2,1)S(1)}, bf16[256,768]{0,1:T(8,128)(2,1)S(1)}, u32[]{:S(2)}, u32[]{:S(2)}) collective-permute-start(bf16[256,768]{0,1:T(8,128)(2,1)S(1)} %bitcast.251), channel_id=1, source_target_pairs={{0,2},{1,3},{2,0},{3,1},{4,6},{5,7},{6,4},{7,5},{8,10},{9,11},{10,... | collective-permute-start | bytes 1179656 | tf_op jit(solution)/shard_map/ppermute | solution.py:593
  (29 other events, 89.5 us)
